TPU v7x, 512 devices: a whole 4x8x8 slice. The times are simulated.
512 devices in a mesh: seq: 16 (over z, core), fsdp: 32 (over y, x).
Axes of the slice: x: 4, y: 8, z: 8, core: 2. Of those that a mesh axis runs over, the one named last changes fastest.
Arguments:
- latents: bfloat16 [32, 2048, 2432], P('fsdp', 'seq'), may hold values from -6 to 6
- noise: bfloat16 [32, 2048, 2432], P('fsdp', 'seq'), may hold values from -6 to 6
- timesteps: int32 [32], P('fsdp'), may hold values from 1 to 999
- time_weight: bfloat16 [256, 4864], P(None, 'fsdp'), may hold values from -0.375 to 0.375
- qkv_weight: bfloat16 [2432, 3, 2048], P(None, None, 'seq'), may hold values from -0.125 to 0.125
- cached_targets: bfloat16 [16384, 2048], P('fsdp', 'seq'), may hold values from -6 to 6
- cache_owner: int32 [16384, 1], P('fsdp'), may hold values from 0 to 31; in each aligned block of 512 rows (0 to 511, 512 to 1023, ...) at most 32 rows name the same one
- cache_pos: int32 [16384], P('fsdp'), may hold values from 0 to 2047
Outputs:
- critic_grad: bfloat16 [32, 2048, 2048], P('fsdp', None, 'seq')
Inputs may be any that keep to these rules, and one draw needn't show every extreme that they name: `cache_owner`: in the rows of one index of fsdp (512 aligned rows) no sample is named more than 32 times, a bound that some block reaches.
All inputs are finite; a program needn't handle non-finite values.
Results may differ from a plain program's by a relative error of at most 0.012.
Values may be sent and summed in bfloat16 or wider, within the bound.
No kernel may reach another device: no remote copies, remote signals or barrier semaphores. Data moves between devices by JAX's collectives and lax.ppermute only.
A program may use at most 64 MiB of HBM per device.

v0:
```python
import math

import jax
import jax.numpy as jnp
from jax import lax
from jax.sharding import PartitionSpec as P

HEAD_DIM = 64
FREQ = 256


def embed_times(stamps):
    half = FREQ // 2
    steps = jnp.arange(half, dtype=jnp.float32)
    freqs = jnp.exp(-math.log(10000.0) * steps / half)
    angles = stamps.astype(jnp.float32)[:, None] * freqs[None, :]
    raw = jnp.concatenate([jnp.cos(angles), jnp.sin(angles)], axis=1)
    return jax.nn.silu(raw).astype(jnp.bfloat16)


def place_sums(rows, places, length):
    onehot = (places[:, None] == jnp.arange(length, dtype=jnp.int32)[None, :]).astype(jnp.bfloat16)
    sums = jnp.einsum("rp,rw->pw", onehot, rows, preferred_element_type=jnp.float32)
    tally = jnp.sum(onehot.astype(jnp.float32), axis=0)
    return (sums, tally)


def earlier_rows(crows):
    order = jnp.arange(crows, dtype=jnp.int32)
    return (order[:, None] > order[None, :]).astype(jnp.bfloat16)


def shards(
    latents, noise, timesteps, time_weight, qkv_weight, cached_targets, cache_owner, cache_pos
):
    dmodel = latents.shape[2]
    embed = embed_times(timesteps)
    modulation = jnp.dot(
        embed,
        lax.all_gather(time_weight, "fsdp", axis=1, tiled=True),
        preferred_element_type=jnp.float32,
    )
    shift = modulation[:, :dmodel]
    scale = modulation[:, dmodel:]
    sigma = timesteps.astype(jnp.float32)[0] / 1000.0
    noised = (1.0 - sigma) * latents[0].astype(jnp.float32) + sigma * noise[0].astype(jnp.float32)
    center = jnp.mean(noised, axis=1, keepdims=True)
    spread = jnp.mean((noised - center) ** 2, axis=1, keepdims=True)
    normed = (noised - center) / jnp.sqrt(spread + 1e-06)
    modulated = (normed * (1.0 + scale) + shift).astype(jnp.bfloat16)
    width = qkv_weight.shape[2]
    flat_weight = qkv_weight.reshape(dmodel, 3 * width)
    qkv = jnp.dot(
        lax.all_gather(modulated, "seq", axis=0, tiled=True),
        flat_weight,
        preferred_element_type=jnp.float32,
    ).astype(jnp.bfloat16)
    length = qkv.shape[0]
    heads = width // HEAD_DIM
    query = qkv[:, :width].reshape(length, heads, HEAD_DIM)
    keys = qkv[:, width : 2 * width].reshape(length, heads, HEAD_DIM)
    values = qkv[:, 2 * width :].reshape(length, heads, HEAD_DIM)
    block = min(512, length)
    query_blocks = query.reshape(length // block, block, heads, HEAD_DIM)

    def attend(rows):
        scores = jnp.einsum(
            "qhd,khd->hqk", rows, keys, preferred_element_type=jnp.float32
        ) / math.sqrt(HEAD_DIM)
        probs = jax.nn.softmax(scores, axis=-1).astype(jnp.bfloat16)
        return jnp.einsum("hqk,khd->qhd", probs, values, preferred_element_type=jnp.float32)

    attended = lax.map(attend, query_blocks).reshape(length, width)
    my_sample = lax.axis_index("fsdp")
    samples = lax.axis_size("fsdp")
    crows = cached_targets.shape[0]
    slots = 2 * crows // samples
    strict = earlier_rows(crows)
    slot_ids = jnp.arange(slots, dtype=jnp.int32)

    def one_block(acc, item):
        target_rows, owners, places = item
        mine = (owners == my_sample).astype(jnp.bfloat16)
        before = jnp.dot(strict, mine[:, None], preferred_element_type=jnp.float32)[:, 0].astype(
            jnp.int32
        )
        select = ((mine[None, :] > 0) & (before[None, :] == slot_ids[:, None])).astype(jnp.bfloat16)
        picked = jnp.dot(select, target_rows, preferred_element_type=jnp.float32).astype(
            jnp.bfloat16
        )
        picked_places = jnp.dot(
            select.astype(jnp.float32),
            places.astype(jnp.float32)[:, None],
            precision=lax.Precision.HIGHEST,
        )[:, 0]
        filled = jnp.sum(select.astype(jnp.float32), axis=1)
        where_to = jnp.where(filled > 0.5, picked_places.astype(jnp.int32), length)
        sums, tally = place_sums(picked, where_to, length)
        return ((acc[0] + sums, acc[1] + tally), None)

    start_sums = (jnp.zeros((length, width), jnp.float32), jnp.zeros((length,), jnp.float32))
    carry = start_sums
    target_rows = lax.all_gather(cached_targets, "fsdp", axis=0, tiled=True)
    owners = lax.all_gather(cache_owner, "fsdp", axis=0, tiled=True)
    places = lax.all_gather(cache_pos, "fsdp", axis=0, tiled=True)
    blocks = target_rows.shape[0] // crows
    items = (
        target_rows.reshape(blocks, crows, width),
        owners.reshape(blocks, crows),
        places.reshape(blocks, crows),
    )
    carry, unused = lax.scan(one_block, carry, items)
    target_sum, count = carry
    result = count[:, None] * attended - target_sum
    return result.astype(jnp.bfloat16).reshape(1, length, width)


def solution(mesh):
    placed = (
        P("fsdp", "seq", None),
        P("fsdp", "seq", None),
        P("fsdp"),
        P(None, "fsdp"),
        P(None, None, "seq"),
        P("fsdp", "seq"),
        P("fsdp", None),
        P("fsdp"),
    )
    return jax.shard_map(
        shards, mesh=mesh, in_specs=placed, out_specs=P("fsdp", None, "seq"), check_vma=False
    )
```

profile of v0, /device:TPU:1, one launch (start us, length us, event | category | flops | bytes accessed | tf_op | source)
XLA Modules:
  0.0 338.6 jit_solution(14839895765454153978)
XLA Ops:
  8.9 4.1 %copy.21 = bf16[2432,3,128]{0,2,1:T(8,128)(2,1)} copy(bf16[2432,3,128]{2,0,1:T(8,128)(2,1)} %param.16) | data formatting | bytes 3735552 | tf_op args[4]
  12.9 39.3 %all_gather.15 = s32[16384,1]{0,1:T(1,128)S(1)} all-gather(s32[512,1]{0,1:T(1,128)S(1)} %copy-done.3), channel_id=1, replica_groups=mesh['seq'=16,'fsdp'=32] {'fsdp'}, dimensions={0}, use_global_device_ids=true | all-gather | bytes 67584 | tf_op jit(solution)/shard_map/all_gather | solution.py:104
  53.4 36.7 %all-gather = s32[32,1,512]{2,1,0:T(1,128)S(1)} all-gather(s32[1,1,512]{2,1,0:T(1,128)S(1)} %bitcast.93), channel_id=1, replica_groups=mesh['seq'=16,'fsdp'=32] {'fsdp'}, dimensions={0}, use_global_device_ids=true | all-gather | bytes 67584 | tf_op jit(solution)/shard_map/all_gather | solution.py:105
  91.0 5.7 %all-gather.7.cloned.1.call-done = bf16[256,4864]{0,1:T(8,128)(2,1)} async-done(((bf16[256,152]{0,1:T(8,128)(2,1)}), bf16[256,4864]{0,1:T(8,128)(2,1)}) %all-gather.7.cloned.1.call-update) | async-done | bytes 2490384 | tf_op jit(solution)/shard_map/all_gather | solution.py:40
  96.6 2.5 fusion.72
  100.5 84.7 %all-gather.5.cloned.1.call-done = bf16[16384,128]{1,0:T(8,128)(2,1)} async-done(((bf16[512,128]{1,0:T(8,128)(2,1)}), bf16[16384,128]{1,0:T(8,128)(2,1)}) %all-gather.5.cloned.1.call-update) | async-done | bytes 4194320 | tf_op jit(solution)/shard_map/all_gather | solution.py:103
  185.1 75.6 %while.24 = (s32[]{:T(128)}, f32[2048,128]{1,0:T(8,128)S(1)}, f32[2048]{0:T(1024)S(1)}, s32[32,512]{1,0:T(8,128)S(1)}, s32[]{:T(128)}, /*index=5*/s32[32,512]{1,...) while((s32[]{:T(128)}, f32[2048,128]{1,0:T(8,128)S(1)}, f32[2048]{0:T(1024)S(1)}, ...), condition=%wide.region_3.4_spmd.clone, body=%wide.region_0.3_spmd.clone.sunk | while | flops 23225412 | bytes 2283132 | solution.py:112
  185.7 1.7 convolution_add_fusion.2
  188.0 1.7 convolution_add_fusion.2
  190.4 1.7 convolution_add_fusion.2
  192.8 1.7 convolution_add_fusion.2
  195.1 1.7 convolution_add_fusion.2
  197.5 1.7 convolution_add_fusion.2
  199.8 1.7 convolution_add_fusion.2
  202.2 1.7 convolution_add_fusion.2
  204.6 1.7 convolution_add_fusion.2
  209.3 1.7 convolution_add_fusion.2
  211.6 1.7 convolution_add_fusion.2
  214.0 1.7 convolution_add_fusion.2
  218.7 1.7 convolution_add_fusion.2
  223.5 1.7 convolution_add_fusion.2
  225.8 1.7 convolution_add_fusion.2
  228.2 1.7 convolution_add_fusion.2
  230.6 1.7 convolution_add_fusion.2
  233.0 1.7 convolution_add_fusion.2
  235.3 1.7 convolution_add_fusion.2
  237.7 1.7 convolution_add_fusion.2
  240.1 1.7 convolution_add_fusion.2
  242.4 1.7 convolution_add_fusion.2
  244.8 1.7 convolution_add_fusion.2
  247.1 1.7 convolution_add_fusion.2
  249.5 1.7 convolution_add_fusion.2
  254.2 1.7 convolution_add_fusion.2
  256.6 1.7 convolution_add_fusion.2
  261.1 8.6 %convolution_convert_fusion.1 = bf16[2048,384]{0,1:T(8,128)(2,1)S(1)} fusion(bf16[2048,2432]{1,0:T(8,128)(2,1)} %all-gather.9.cloned.1.call-done, bf16[2432,384]{0,1:T(8,128)(2,1)} %bitcast.86), kind=kOutput, calls=%fused_computation.53 | convolution fusion | flops 3825991680 | bytes 13402112 | tf_op jit(solution)/shard_map/dot_general | solution.py:53
  272.2 58.3 %while.23 = (s32[]{:T(128)}, f32[4,512,2,64]{1,0,3,2:T(4,128)S(1)}, bf16[4,512,2,64]{1,3,2,0:T(8,128)(2,1)}, bf16[2048,2,64]{0,2,1:T(8,128)(2,1)}, bf16[2048,2,64]{0,2,1:T(8,128)(2,1)}, /*index=5*/s32[]{:T(128)}, s32[]{:T(128)}) while((s32[]{:T(128)}, f32[4,512,2,64]{1,0,3,2:T(4,128)S(1)}, bf16[4,512,2,64]{1,3,2,0:T(8,128)(2,1)}, ...), condition=%wide.region_9.10_spmd, body=%wide.region_6.9_spmd.sunk | while | flops 547358720 | bytes 21373548 | solution.py:73
  272.2 6.9 %fusion.95 = (f32[2,512]{1,0:T(2,128)S(1)}, f32[2,512,2048]{2,1,0:T(8,128)}) fusion(bf16[2048,2,64]{0,2,1:T(8,128)(2,1)} %get-tuple-element.286, bf16[4,512,2,64]{1,3,2,0:T(8,128)(2,1)} %get-tuple-element.285, s32[]{:T(128)} %get-tuple-element.276), kind=kOutput, calls=%fused_computation.73.clone.1 | convolution fusion | flops 274728960 | bytes 9048576 | tf_op jit(solution)/shard_map/while/body/eval_jaxpr/sub | solution.py:70
  279.1 4.8 %fusion.96 = f32[1,512,2,64]{1,3,2,0:T(8,128)S(1)} fusion(bf16[2048,2,64]{0,2,1:T(8,128)(2,1)S(1)} %copy-done.2, f32[2,512,2048]{2,1,0:T(8,128)} %get-tuple-element.233, f32[2,512]{1,0:T(2,128)S(1)} %get-tuple-element.234), kind=kOutput, calls=%fused_computation.9.clone.1 | convolution fusion | flops 272629760 | bytes 9179136 | tf_op jit(solution)/shard_map/while/body/eval_jaxpr/hqk,khd->qhd/dot_general | solution.py:71
  284.2 2.5 dynamic_update_slice.5
  286.8 6.9 %fusion.95 = (f32[2,512]{1,0:T(2,128)S(1)}, f32[2,512,2048]{2,1,0:T(8,128)}) fusion(bf16[2048,2,64]{0,2,1:T(8,128)(2,1)} %get-tuple-element.286, bf16[4,512,2,64]{1,3,2,0:T(8,128)(2,1)} %get-tuple-element.285, s32[]{:T(128)} %get-tuple-element.276), kind=kOutput, calls=%fused_computation.73.clone.1 | convolution fusion | flops 274728960 | bytes 9048576 | tf_op jit(solution)/shard_map/while/body/eval_jaxpr/sub | solution.py:70
  293.7 4.8 %fusion.96 = f32[1,512,2,64]{1,3,2,0:T(8,128)S(1)} fusion(bf16[2048,2,64]{0,2,1:T(8,128)(2,1)S(1)} %copy-done.2, f32[2,512,2048]{2,1,0:T(8,128)} %get-tuple-element.233, f32[2,512]{1,0:T(2,128)S(1)} %get-tuple-element.234), kind=kOutput, calls=%fused_computation.9.clone.1 | convolution fusion | flops 272629760 | bytes 9179136 | tf_op jit(solution)/shard_map/while/body/eval_jaxpr/hqk,khd->qhd/dot_general | solution.py:71
  298.8 2.5 dynamic_update_slice.5
  301.4 6.9 %fusion.95 = (f32[2,512]{1,0:T(2,128)S(1)}, f32[2,512,2048]{2,1,0:T(8,128)}) fusion(bf16[2048,2,64]{0,2,1:T(8,128)(2,1)} %get-tuple-element.286, bf16[4,512,2,64]{1,3,2,0:T(8,128)(2,1)} %get-tuple-element.285, s32[]{:T(128)} %get-tuple-element.276), kind=kOutput, calls=%fused_computation.73.clone.1 | convolution fusion | flops 274728960 | bytes 9048576 | tf_op jit(solution)/shard_map/while/body/eval_jaxpr/sub | solution.py:70
  308.3 4.8 %fusion.96 = f32[1,512,2,64]{1,3,2,0:T(8,128)S(1)} fusion(bf16[2048,2,64]{0,2,1:T(8,128)(2,1)S(1)} %copy-done.2, f32[2,512,2048]{2,1,0:T(8,128)} %get-tuple-element.233, f32[2,512]{1,0:T(2,128)S(1)} %get-tuple-element.234), kind=kOutput, calls=%fused_computation.9.clone.1 | convolution fusion | flops 272629760 | bytes 9179136 | tf_op jit(solution)/shard_map/while/body/eval_jaxpr/hqk,khd->qhd/dot_general | solution.py:71
  313.4 2.5 dynamic_update_slice.5
  316.0 6.9 %fusion.95 = (f32[2,512]{1,0:T(2,128)S(1)}, f32[2,512,2048]{2,1,0:T(8,128)}) fusion(bf16[2048,2,64]{0,2,1:T(8,128)(2,1)} %get-tuple-element.286, bf16[4,512,2,64]{1,3,2,0:T(8,128)(2,1)} %get-tuple-element.285, s32[]{:T(128)} %get-tuple-element.276), kind=kOutput, calls=%fused_computation.73.clone.1 | convolution fusion | flops 274728960 | bytes 9048576 | tf_op jit(solution)/shard_map/while/body/eval_jaxpr/sub | solution.py:70
  322.8 4.8 %fusion.96 = f32[1,512,2,64]{1,3,2,0:T(8,128)S(1)} fusion(bf16[2048,2,64]{0,2,1:T(8,128)(2,1)S(1)} %copy-done.2, f32[2,512,2048]{2,1,0:T(8,128)} %get-tuple-element.233, f32[2,512]{1,0:T(2,128)S(1)} %get-tuple-element.234), kind=kOutput, calls=%fused_computation.9.clone.1 | convolution fusion | flops 272629760 | bytes 9179136 | tf_op jit(solution)/shard_map/while/body/eval_jaxpr/hqk,khd->qhd/dot_general | solution.py:71
  328.0 2.5 dynamic_update_slice.5
  (279 shorter events, 39.7 us)
Async XLA Ops:
  6.5 90.1 %all-gather.7.cloned.1.call-start = ((), (), s32[]{:S(2)}) async-start(), calls=%async_computation.1 | async-start | bytes 2568192 | tf_op jit(solution)/shard_map/all_gather | solution.py:40
  7.3 177.9 %all-gather.5.cloned.1.call-start = ((), (), s32[]{:S(2)}) async-start(), calls=%async_computation | async-start | bytes 4325376 | tf_op jit(solution)/shard_map/all_gather | solution.py:103
  8.0 253.1 %all-gather.9.cloned.1.call-start = ((), (), s32[]{:S(2)}) async-start(), calls=%async_computation.2 | async-start | bytes 10584064 | tf_op jit(solution)/shard_map/all_gather | solution.py:54
  8.8 4.1 %copy-start.3 = (s32[512,1]{0,1:T(1,128)S(1)}, s32[512,1]{0,1:T(1,128)}, u32[]{:S(2)}) copy-start(s32[512,1]{0,1:T(1,128)} %param.18) | copy-start | bytes 6148
  8.8 44.6 %copy-start.4 = (s32[512]{0:T(512)S(1)}, s32[512]{0:T(512)}, u32[]{:S(2)}) copy-start(s32[512]{0:T(512)} %param.19) | copy-start | bytes 6148
  8.8 81.3 %copy-start = (bf16[1,128,2432]{2,1,0:T(8,128)(2,1)S(1)}, bf16[1,128,2432]{2,1,0:T(8,128)(2,1)}, u32[]{:S(2)}) copy-start(bf16[1,128,2432]{2,1,0:T(8,128)(2,1)} %param.13) | copy-start | bytes 1867780
  8.9 81.3 %copy-start.1 = (bf16[1,128,2432]{2,1,0:T(8,128)(2,1)S(1)}, bf16[1,128,2432]{2,1,0:T(8,128)(2,1)}, u32[]{:S(2)}) copy-start(bf16[1,128,2432]{2,1,0:T(8,128)(2,1)} %param.12) | copy-start | bytes 1867780
  272.2 6.9 %copy-start.2 = (bf16[2048,2,64]{0,2,1:T(8,128)(2,1)S(1)}, bf16[2048,2,64]{0,2,1:T(8,128)(2,1)}, u32[]{:S(2)}) copy-start(bf16[2048,2,64]{0,2,1:T(8,128)(2,1)} %get-tuple-element.287) | copy-start | bytes 1572868 | tf_op jit(solution)/shard_map/while
  286.8 6.9 %copy-start.2 = (bf16[2048,2,64]{0,2,1:T(8,128)(2,1)S(1)}, bf16[2048,2,64]{0,2,1:T(8,128)(2,1)}, u32[]{:S(2)}) copy-start(bf16[2048,2,64]{0,2,1:T(8,128)(2,1)} %get-tuple-element.287) | copy-start | bytes 1572868 | tf_op jit(solution)/shard_map/while
  301.4 6.9 %copy-start.2 = (bf16[2048,2,64]{0,2,1:T(8,128)(2,1)S(1)}, bf16[2048,2,64]{0,2,1:T(8,128)(2,1)}, u32[]{:S(2)}) copy-start(bf16[2048,2,64]{0,2,1:T(8,128)(2,1)} %get-tuple-element.287) | copy-start | bytes 1572868 | tf_op jit(solution)/shard_map/while
  315.9 6.9 %copy-start.2 = (bf16[2048,2,64]{0,2,1:T(8,128)(2,1)S(1)}, bf16[2048,2,64]{0,2,1:T(8,128)(2,1)}, u32[]{:S(2)}) copy-start(bf16[2048,2,64]{0,2,1:T(8,128)(2,1)} %get-tuple-element.287) | copy-start | bytes 1572868 | tf_op jit(solution)/shard_map/while
Sparse Core Ops, SparseCore 0:
  10.5 86.0 all-gather.6
  99.8 85.2 all-gather.4
  187.3 67.5 all-gather.8
where the time goes:
time: 342 us; the launch traced here: 339 us
  matrix products  123 us (36%)
  waiting for transfers between devices  91.8 us (27%)
  blocking collectives  76 us (22%)
  local copies, waits for them, and re-layouts  20 us (6%)
  between operations  14 us (4%)
  other arithmetic  12.6 us (4%)
    all_gather x1, waiting for transfers between devices, shards(): target_rows = lax.all_gather(cached_targets, 'fsdp', axis=0, tiled=True)  84.7 us
    dot_general x32, matrix products, place_sums(): jnp.einsum('rp,rw->pw', onehot, rows, preferred_element_type=jnp.float32)  53.4 us
    all_gather x1, blocking collectives, shards(): owners = lax.all_gather(cache_owner, 'fsdp', axis=0, tiled=True)  39.3 us
    all_gather x1, blocking collectives, shards(): places = lax.all_gather(cache_pos, 'fsdp', axis=0, tiled=True)  36.7 us
    sub x4, matrix products, attend(): probs = jax.nn.softmax(scores, axis=-1).astype(jnp.bfloat16)  27.5 us
    dot_general x4, matrix products, attend(): jnp.einsum('hqk,khd->qhd', probs, values, preferred_element_type=jnp.floa...  19.3 us
    dynamic_update_slice x8, local copies, waits for them, and re-layouts, shards(): attended = lax.map(attend, query_blocks).reshape(length, width)  11.3 us
    dot_general x1, matrix products, shards(): jnp.dot(lax.all_gather(modulated, 'seq', axis=0, tiled=True), flat_weight...  8.59 us
  transfers between devices with their start and end apart: 3, of which 2 were waited for; matrix products, arithmetic and copies ran while one was open for 25% of the time, Pallas kernels for 0%

commit v1 on v0

v1 whole, which is shorter than its diff:
```python
import functools
import math

import jax
import jax.numpy as jnp
from jax import lax
from jax.experimental import pallas as pl
from jax.experimental.pallas import tpu as pltpu
from jax.sharding import PartitionSpec as P

HEAD_DIM = 64
FREQ = 256
F32 = jnp.float32
BF16 = jnp.bfloat16


def embed_times(stamps):
    half = FREQ // 2
    steps = jnp.arange(half, dtype=F32)
    freqs = jnp.exp(-math.log(10000.0) * steps / half)
    angles = stamps.astype(F32)[:, None] * freqs[None, :]
    raw = jnp.concatenate([jnp.cos(angles), jnp.sin(angles)], axis=1)
    return jax.nn.silu(raw).astype(BF16)


def norm_kernel(stamp_ref, latents_ref, noise_ref, out_ref):
    sigma = stamp_ref[0].astype(F32) / 1000.0
    noised = (1.0 - sigma) * latents_ref[...].astype(F32) + sigma * noise_ref[...].astype(F32)
    center = jnp.mean(noised, axis=1, keepdims=True)
    shifted = noised - center
    spread = jnp.mean(shifted * shifted, axis=1, keepdims=True)
    out_ref[...] = (shifted / jnp.sqrt(spread + 1e-06)).astype(BF16)


def normalize(timesteps, latents, noise):
    rows, dmodel = latents.shape
    block = 32
    spec = pl.BlockSpec((block, dmodel), lambda i: (i, 0))
    return pl.pallas_call(
        norm_kernel,
        grid=(rows // block,),
        in_specs=[pl.BlockSpec(memory_space=pltpu.SMEM), spec, spec],
        out_specs=spec,
        out_shape=jax.ShapeDtypeStruct((rows, dmodel), BF16),
        name="normalize",
    )(timesteps, latents, noise)


def pack_rows(targets, owners, places, timesteps, samples):
    crows, width = targets.shape
    slots = 32
    sample_ids = jnp.arange(samples, dtype=jnp.int32)
    owned = owners[:, None] == sample_ids[None, :]
    order = jnp.arange(crows, dtype=jnp.int32)
    strict = (order[:, None] > order[None, :]).astype(BF16)
    before = jnp.dot(strict, owned.astype(BF16), preferred_element_type=F32)
    rank = jnp.sum(jnp.where(owned, before, 0.0), axis=1).astype(jnp.int32)
    slot = owners * slots + rank
    select = (jnp.arange(samples * slots, dtype=jnp.int32)[:, None] == slot[None, :]).astype(BF16)
    rows = jnp.dot(select, targets, preferred_element_type=F32).astype(BF16)
    ranked = rank[:, None] == jnp.arange(slots, dtype=jnp.int32)[None, :]
    high = (places // 64 + 1).astype(F32)[:, None]
    low = (places % 64).astype(F32)[:, None]
    coded = jnp.concatenate([jnp.where(ranked, high, 0.0), jnp.where(ranked, low, 0.0)], axis=1)
    where_to = jnp.einsum(
        "rs,rc->sc", owned.astype(BF16), coded.astype(BF16), preferred_element_type=F32
    )
    stamp = jnp.broadcast_to(
        jnp.concatenate([timesteps // 32, timesteps % 32]).astype(F32)[None, :], (samples, 2)
    )
    extra = jnp.concatenate(
        [where_to, stamp, jnp.zeros((samples, width - 2 * slots - 2), F32)], axis=1
    ).astype(BF16)
    extra = jnp.broadcast_to(extra[:, None, :], (samples, 16, width))
    return jnp.concatenate([rows.reshape(samples, slots, width), extra], axis=1)


def attend_kernel(
    x_ref, weight_ref, bias_ref, column_ref, row_ref, target_ref, out_ref,
    key_ref, first_ref, second_ref, query_ref, diff_ref,
):
    step = pl.program_id(0)
    block = x_ref.shape[0]
    slots, width = query_ref.shape
    length = key_ref.shape[0]
    here = pl.ds(pl.multiple_of(step * block, block), block)
    qkv = jnp.dot(x_ref[...], weight_ref[...], preferred_element_type=F32) + bias_ref[...]
    qkv = qkv.astype(BF16)
    left = lax.broadcasted_iota(jnp.int32, (block, width), 1) < HEAD_DIM
    one = jnp.ones((block, width), BF16)
    key_ref[here, :] = qkv[:, width : 2 * width]
    value = qkv[:, 2 * width :]
    first_ref[here, :] = jnp.where(left, value, one)
    second_ref[here, :] = jnp.where(left, one, value)
    spots = lax.broadcasted_iota(jnp.int32, (slots, block), 1) + step * block
    pick = (column_ref[...] == spots).astype(F32).astype(BF16)
    picked = jnp.dot(pick, qkv[:, :width], preferred_element_type=F32)

    @pl.when(step == 0)
    def _():
        query_ref[...] = picked

    @pl.when(step > 0)
    def _():
        query_ref[...] += picked

    @pl.when(step == pl.num_programs(0) - 1)
    def _():
        factor = math.log2(math.e) / math.sqrt(HEAD_DIM)
        part = 256
        half = lax.broadcasted_iota(jnp.int32, (part, width), 1) < HEAD_DIM
        for start in range(0, slots, part):
            query = query_ref[start : start + part, :]
            outs = []
            for keep, value_ref in ((half, first_ref), (~half, second_ref)):
                mine = jnp.where(keep, query, 0.0).astype(BF16)
                scores = lax.dot_general(
                    mine, key_ref[...], (((1,), (1,)), ((), ())), preferred_element_type=F32
                )
                top = jnp.max(scores, axis=1, keepdims=True)
                probs = jnp.exp2((scores - top) * factor).astype(BF16)
                mixed = jnp.dot(probs, value_ref[...], preferred_element_type=F32)
                outs.append(mixed / pltpu.roll(mixed, HEAD_DIM, 1))
            attended = jnp.where(half, outs[0], outs[1])
            target = target_ref[start : start + part, :].astype(F32)
            diff_ref[start : start + part, :] = (attended - target).astype(BF16)
        for start in range(0, length, part):
            spots = lax.broadcasted_iota(jnp.int32, (part, slots), 0) + start
            spread = (row_ref[...] == spots).astype(F32).astype(BF16)
            out_ref[start : start + part, :] = jnp.dot(
                spread, diff_ref[...], preferred_element_type=F32
            ).astype(BF16)


def attend(tokens, weight, bias, spots, targets):
    length, dmodel = tokens.shape
    slots, width = targets.shape
    block = 256
    whole = lambda shape: pl.BlockSpec(shape, lambda i: (0, 0))
    return pl.pallas_call(
        attend_kernel,
        grid=(length // block,),
        in_specs=[
            pl.BlockSpec((block, dmodel), lambda i: (i, 0)),
            whole((dmodel, 3 * width)),
            whole((1, 3 * width)),
            whole((slots, 1)),
            whole((1, slots)),
            whole((slots, width)),
        ],
        out_specs=whole((length, width)),
        out_shape=jax.ShapeDtypeStruct((length, width), BF16),
        scratch_shapes=[
            pltpu.VMEM((length, width), BF16),
            pltpu.VMEM((length, width), BF16),
            pltpu.VMEM((length, width), BF16),
            pltpu.VMEM((slots, width), F32),
            pltpu.VMEM((slots, width), BF16),
        ],
        compiler_params=pltpu.CompilerParams(vmem_limit_bytes=48 * 1024 * 1024),
        name="attend",
    )(tokens, weight, bias, spots.reshape(slots, 1), spots.reshape(1, slots), targets)


def shards(
    latents, noise, timesteps, time_weight, qkv_weight, cached_targets, cache_owner, cache_pos
):
    dmodel = latents.shape[2]
    width = qkv_weight.shape[2]
    samples = lax.axis_size("fsdp")
    slots = 32
    normed = normalize(timesteps, latents[0], noise[0])
    tokens = lax.all_gather(normed, "seq", axis=0, tiled=True)
    sent = pack_rows(cached_targets, cache_owner[:, 0], cache_pos, timesteps, samples)
    got = lax.all_to_all(sent, "fsdp", 0, 0, tiled=True)
    targets = got[:, :slots].reshape(samples * slots, width)
    extra = got[:, slots].astype(F32)
    high, low = extra[:, :slots], extra[:, slots : 2 * slots]
    spots = jnp.where(high > 0.5, (high - 1.0) * 64.0 + low, -1.0).astype(jnp.int32)
    stamps = (extra[:, 2 * slots] * 32.0 + extra[:, 2 * slots + 1]).astype(jnp.int32)
    part = jnp.dot(embed_times(stamps), time_weight, preferred_element_type=F32)
    modulation = lax.all_to_all(part, "fsdp", 0, 0, tiled=True).reshape(2 * dmodel)
    shift = modulation[:dmodel]
    scale = modulation[dmodel:]
    flat_weight = qkv_weight.reshape(dmodel, 3 * width).astype(F32)
    weight = ((1.0 + scale)[:, None] * flat_weight).astype(BF16)
    bias = jnp.sum(shift[:, None] * flat_weight, axis=0, keepdims=True)
    return attend(tokens, weight, bias, spots, targets)[None]


def solution(mesh):
    placed = (
        P("fsdp", "seq", None),
        P("fsdp", "seq", None),
        P("fsdp"),
        P(None, "fsdp"),
        P(None, None, "seq"),
        P("fsdp", "seq"),
        P("fsdp", None),
        P("fsdp"),
    )
    return jax.shard_map(
        shards, mesh=mesh, in_specs=placed, out_specs=P("fsdp", None, "seq"), check_vma=False
    )
```

time: 342 us -> 111 us (0.32)
  matrix products: 123 us -> 2.45 us
  blocking collectives: 76 us -> 0 us
  waiting for transfers between devices: 91.8 us -> 41.6 us
  Pallas kernels: 0 us -> 23.1 us
  starting transfers between devices: 0.08 us -> 15.7 us
  local copies, waits for them, and re-layouts: 20 us -> 7.25 us
  other arithmetic: 12.6 us -> 5.71 us
    dot_general x102 -> x4, matrix products: 95.2 us -> 2.45 us  [the longest x1 1.03 us: pack_rows(): before = jnp.dot(strict, owned.astype(BF16), preferred_element_type=F32)]
    all_gather x2 -> x0, blocking collectives: 76 us -> none  [the longest x1 39.3 us: shards(): owners = lax.all_gather(cache_owner, 'fsdp', axis=0, tiled=True)]
    all_gather x3 -> x1, waiting for transfers between devices: 90.4 us -> 25.5 us  [shards(): tokens = lax.all_gather(normed, 'seq', axis=0, tiled=True)]
    sub x4 -> x0, matrix products: 27.5 us -> none  [attend(): probs = jax.nn.softmax(scores, axis=-1).astype(jnp.bfloat16)]
    pallas_call x0 -> x2, Pallas kernels: none -> 23.1 us  [the longest x1 19.2 us: attend(): pl.pallas_call(attend_kernel, grid=(length // block,), in_specs=[pl.Block...]
    all_to_all x0 -> x2, waiting for transfers between devices: none -> 16 us  [the longest x1 8.21 us: shards(): got = lax.all_to_all(sent, 'fsdp', 0, 0, tiled=True)]
    all_to_all x0 -> x2, starting transfers between devices: none -> 15.7 us  [the longest x1 10.5 us: shards(): got = lax.all_to_all(sent, 'fsdp', 0, 0, tiled=True)]
    dynamic_update_slice x8 -> x0, local copies, waits for them, and re-layouts: 11.3 us -> none  [shards(): attended = lax.map(attend, query_blocks).reshape(length, width)]
  transfers between devices with their start and end apart: 3 -> 3, of which waited for: 2 -> 3; matrix products, arithmetic and copies ran while one was open for 25% -> 14% of each run, Pallas kernels for 0% -> 0%
where the time goes in v1:
time: 111 us; the launch traced here: 110 us
  waiting for transfers between devices  41.6 us (37%)
  Pallas kernels  23.1 us (21%)
  starting transfers between devices  15.7 us (14%)
  between operations  14.3 us (13%)
  local copies, waits for them, and re-layouts  7.25 us (7%)
  other arithmetic  5.71 us (5%)
  matrix products  2.45 us (2%)
    all_gather x1, waiting for transfers between devices, shards(): tokens = lax.all_gather(normed, 'seq', axis=0, tiled=True)  25.5 us
    pallas_call x1, Pallas kernels, attend(): pl.pallas_call(attend_kernel, grid=(length // block,), in_specs=[pl.Block...  19.2 us
    all_to_all x1, starting transfers between devices, shards(): got = lax.all_to_all(sent, 'fsdp', 0, 0, tiled=True)  10.5 us
    all_to_all x1, waiting for transfers between devices, shards(): got = lax.all_to_all(sent, 'fsdp', 0, 0, tiled=True)  8.21 us
    all_to_all x1, waiting for transfers between devices, shards(): lax.all_to_all(part, 'fsdp', 0, 0, tiled=True).reshape(2 * dmodel)  7.79 us
    all_to_all x1, starting transfers between devices, shards(): lax.all_to_all(part, 'fsdp', 0, 0, tiled=True).reshape(2 * dmodel)  5.18 us
    pallas_call x1, Pallas kernels, normalize(): pl.pallas_call(norm_kernel, grid=(rows // block,), in_specs=[pl.BlockSpec...  3.87 us
    convert_element_type x1, local copies, waits for them, and re-layouts, shards(): flat_weight = qkv_weight.reshape(dmodel, 3 * width).astype(F32)  2.81 us
  transfers between devices with their start and end apart: 3, of which 3 were waited for; matrix products, arithmetic and copies ran while one was open for 14% of the time, Pallas kernels for 0%

profile of v1, /device:TPU:1, one launch (start us, length us, event | category | flops | bytes accessed | tf_op | source)
XLA Modules:
  0.0 110.0 jit_solution(11659810130560080797)
XLA Ops:
  6.5 0.0 copy-start
  6.5 0.0 all-gather.2.cloned.1.call-start
  7.2 3.9 %normalize.1 = bf16[128,2432]{1,0:T(8,128)(2,1)} custom-call(s32[1]{0:T(128)S(6)} %copy.32.stamp_ref, bf16[128,2432]{1,0:T(8,128)(2,1)} %bitcast.21, bf16[128,2432]{1,0:T(8,128)(2,1)} %bitcast.22), custom_call_target="tpu_custom_call" | custom-call | tf_op jit(solution)/shard_map/normalize/pallas_call | solution.py:39
  11.1 0.0 all-gather.2.cloned.1.call-update
  11.2 1.0 fusion.2
  12.2 0.1 fusion.20
  12.3 0.1 pad.5.clone
  12.4 0.1 pad.6.clone
  12.4 0.7 fusion.17
  13.1 0.7 multiply_add_fusion
  13.8 0.8 convolution_convert_fusion
  14.7 0.0 copy-done
  14.7 0.5 fusion.1
  15.2 0.8 pad_maximum_fusion
  16.0 10.5 %all-to-all-start = ((bf16[32,48,128]{2,1,0:T(8,128)(2,1)}), bf16[32,48,128]{2,1,0:T(8,128)(2,1)S(1)}, u32[]{:S(2)}, u32[]{:S(2)}) async-start(bf16[32,48,128]{2,1,0:T(8,128)(2,1)} %pad_maximum_fusion), calls=%async_computation | async-start | bytes 786432 | tf_op jit(solution)/shard_map/all_to_all | solution.py:175
  26.5 2.8 %copy.26 = bf16[2432,3,128]{0,2,1:T(8,128)(2,1)S(1)} copy(bf16[2432,3,128]{2,0,1:T(8,128)(2,1)} %param.12) | data formatting | bytes 3735552 | tf_op args[4]
  29.2 0.0 copy-start.1
  29.2 2.8 %copy.27 = f32[2432,384]{1,0:T(8,128)} copy(bf16[2432,384]{0,1:T(8,128)(2,1)S(1)} %bitcast.20) | data formatting | bytes 5603328 | tf_op jit(solution)/shard_map/convert_element_type | solution.py:185
  32.1 8.2 %all-to-all-done = bf16[32,48,128]{2,1,0:T(8,128)(2,1)S(1)} async-done(((bf16[32,48,128]{2,1,0:T(8,128)(2,1)}), bf16[32,48,128]{2,1,0:T(8,128)(2,1)S(1)}, u32[]{:S(2)}, u32[]{:S(2)}) %all-to-all-start) | async-done | bytes 393248 | tf_op jit(solution)/shard_map/all_to_all | solution.py:175
  40.3 0.2 fusion.14
  40.5 0.1 multiply_cosine_fusion
  40.6 0.0 copy-done.1
  40.6 0.1 convolution_bitcast_fusion
  40.8 0.7 copy.25
  41.4 5.2 %all-to-all-start.1 = ((f32[32,1,152]{2,1,0:T(1,128)}), f32[32,1,152]{2,1,0:T(1,128)S(1)}, u32[]{:S(2)}, u32[]{:S(2)}) async-start(f32[32,1,152]{2,1,0:T(1,128)} %copy.25), calls=%async_computation.1 | async-start | bytes 65536 | tf_op jit(solution)/shard_map/all_to_all | solution.py:182
  46.6 0.1 fusion.10
  46.7 0.5 reshape.108.column_ref
  47.2 0.1 reshape.104.row_ref
  47.4 7.8 %all-to-all-done.1 = f32[32,1,152]{2,1,0:T(1,128)S(1)} async-done(((f32[32,1,152]{2,1,0:T(1,128)}), f32[32,1,152]{2,1,0:T(1,128)S(1)}, u32[]{:S(2)}, u32[]{:S(2)}) %all-to-all-start.1) | async-done | bytes 19488 | tf_op jit(solution)/shard_map/all_to_all | solution.py:182
  55.1 0.1 slice_reduce_fusion
  55.2 0.1 add.58
  55.3 0.1 mul.75
  55.4 0.5 multiply_reduce_fusion
  55.9 2.5 %multiply_convert_fusion.weight_ref = bf16[2432,384]{1,0:T(8,128)(2,1)S(1)} fusion(f32[2432,384]{1,0:T(8,128)} %copy.27, f32[2432]{0:T(1024)S(1)} %add.58), kind=kLoop, calls=%fused_computation.1 | loop fusion | flops 1867776 | bytes 5613056 | tf_op jit(solution)/shard_map/convert_element_type | solution.py:186
  58.4 25.5 %all-gather.2.cloned.1.call-done.x_ref = bf16[2048,2432]{1,0:T(8,128)(2,1)} async-done(((bf16[128,2432]{1,0:T(8,128)(2,1)}), bf16[2048,2432]{1,0:T(8,128)(2,1)}) %all-gather.2.cloned.1.call-update) | async-done | bytes 9961488 | tf_op jit(solution)/shard_map/all_gather | solution.py:173
  83.9 19.2 %attend.1 = bf16[2048,128]{1,0:T(8,128)(2,1)} custom-call(bf16[2048,2432]{1,0:T(8,128)(2,1)} %all-gather.2.cloned.1.call-done.x_ref, bf16[2432,384]{1,0:T(8,128)(2,1)S(1)} %multiply_convert_fusion.weight_ref, f32[1,384]{1,0:T(1,128)S(1)} %bitcast.19, s32[1024,1]{1,0:T(8,128)S(1)} %reshape.108.column_ref, s32[1,1024]{1,0:T(1,128)S(1)} %reshape.104.row_ref, ...), custom_call_target="tpu_custom_call" | custom-call | tf_op jit(solution)/shard_map/attend/pallas_call | solution.py:140
  (9 shorter events, 0.1 us)
Async XLA Ops:
  6.5 8.1 %copy-start = (bf16[512,128]{1,0:T(8,128)(2,1)S(1)}, bf16[512,128]{1,0:T(8,128)(2,1)}, u32[]{:S(2)}) copy-start(bf16[512,128]{1,0:T(8,128)(2,1)} %param.13) | copy-start | bytes 393220
  6.5 77.4 %all-gather.2.cloned.1.call-start = ((), (), s32[]{:S(2)}) async-start(), calls=%async_computation.2 | async-start | bytes 10584064 | tf_op jit(solution)/shard_map/all_gather | solution.py:173
  16.0 24.3 %all-to-all-start = ((bf16[32,48,128]{2,1,0:T(8,128)(2,1)}), bf16[32,48,128]{2,1,0:T(8,128)(2,1)S(1)}, u32[]{:S(2)}, u32[]{:S(2)}) async-start(bf16[32,48,128]{2,1,0:T(8,128)(2,1)} %pad_maximum_fusion), calls=%async_computation | async-start | bytes 786432 | tf_op jit(solution)/shard_map/all_to_all | solution.py:175
  29.2 11.4 %copy-start.1 = (bf16[256,152]{0,1:T(8,128)(2,1)S(1)}, bf16[256,152]{0,1:T(8,128)(2,1)}, u32[]{:S(2)}) copy-start(bf16[256,152]{0,1:T(8,128)(2,1)} %param.11) | copy-start | bytes 233476
  41.4 13.7 %all-to-all-start.1 = ((f32[32,1,152]{2,1,0:T(1,128)}), f32[32,1,152]{2,1,0:T(1,128)S(1)}, u32[]{:S(2)}, u32[]{:S(2)}) async-start(f32[32,1,152]{2,1,0:T(1,128)} %copy.25), calls=%async_computation.1 | async-start | bytes 65536 | tf_op jit(solution)/shard_map/all_to_all | solution.py:182
Sparse Core Ops, SparseCore 0:
  11.2 72.6 all-gather.1

commit v2 on v1

v2 whole, which is shorter than its diff:
```python
import functools
import math

import jax
import jax.numpy as jnp
from jax import lax
from jax.experimental import pallas as pl
from jax.experimental.pallas import tpu as pltpu
from jax.sharding import PartitionSpec as P

HEAD_DIM = 64
FREQ = 256
SLOTS = 32
MIB = 1024 * 1024
F32 = jnp.float32
BF16 = jnp.bfloat16


def embed_times(stamps):
    half = FREQ // 2
    steps = jnp.arange(half, dtype=F32)
    freqs = jnp.exp(-math.log(10000.0) * steps / half)
    angles = stamps.astype(F32)[:, None] * freqs[None, :]
    raw = jnp.concatenate([jnp.cos(angles), jnp.sin(angles)], axis=1)
    return jax.nn.silu(raw).astype(BF16)


def norm_kernel(stamp_ref, latents_ref, noise_ref, out_ref):
    sigma = stamp_ref[0].astype(F32) / 1000.0
    noised = (1.0 - sigma) * latents_ref[...].astype(F32) + sigma * noise_ref[...].astype(F32)
    center = jnp.mean(noised, axis=1, keepdims=True)
    shifted = noised - center
    spread = jnp.mean(shifted * shifted, axis=1, keepdims=True)
    out_ref[...] = (shifted * lax.rsqrt(spread + 1e-06)).astype(BF16)


def normalize(timesteps, latents, noise):
    rows, dmodel = latents.shape
    block = 64
    spec = pl.BlockSpec((block, dmodel), lambda i: (i, 0))
    return pl.pallas_call(
        norm_kernel,
        grid=(rows // block,),
        in_specs=[pl.BlockSpec(memory_space=pltpu.SMEM), spec, spec],
        out_specs=spec,
        out_shape=jax.ShapeDtypeStruct((rows, dmodel), BF16),
        compiler_params=pltpu.CompilerParams(vmem_limit_bytes=16 * MIB),
        name="normalize",
    )(timesteps, latents, noise)


def onehot(mask):
    return mask.astype(F32).astype(BF16)


def pack_kernel(stamp_ref, owner_ref, place_ref, target_ref, out_ref):
    samples = out_ref.shape[0]
    crows, width = target_ref.shape
    owners = owner_ref[...]
    places = place_ref[...]
    owned = onehot(lax.broadcasted_iota(jnp.int32, (samples, crows), 0) == owners)
    earlier = onehot(
        lax.broadcasted_iota(jnp.int32, (crows, crows), 0)
        < lax.broadcasted_iota(jnp.int32, (crows, crows), 1)
    )
    before = jnp.dot(owned, earlier, preferred_element_type=F32)
    rank = jnp.sum(before * owned.astype(F32), axis=0, keepdims=True).astype(jnp.int32)
    slot = owners * SLOTS + rank
    select = onehot(lax.broadcasted_iota(jnp.int32, (samples * SLOTS, crows), 0) == slot)
    rows = jnp.dot(select, target_ref[...], preferred_element_type=F32).astype(BF16)
    out_ref[:, :SLOTS, :] = rows.reshape(samples, SLOTS, width)
    line = lax.broadcasted_iota(jnp.int32, (width, crows), 0)
    high = (lax.shift_right_logical(places, 6) + 1).astype(F32)
    low = (places & 63).astype(F32)
    coded = jnp.where(line == rank, high, jnp.where(line == rank + SLOTS, low, 0.0)).astype(BF16)
    extra = lax.dot_general(owned, coded, (((1,), (1,)), ((), ())), preferred_element_type=F32)
    lane = lax.broadcasted_iota(jnp.int32, (samples, width), 1)
    stamp = stamp_ref[0]
    upper = lax.shift_right_logical(stamp, 5).astype(F32)
    lower = (stamp & 31).astype(F32)
    extra = jnp.where(lane == 2 * SLOTS, upper, jnp.where(lane == 2 * SLOTS + 1, lower, extra))
    out_ref[:, SLOTS:, :] = jnp.broadcast_to(extra.astype(BF16)[:, None, :], (samples, 16, width))


def pack_rows(timesteps, owners, places, targets, samples):
    vmem = pl.BlockSpec(memory_space=pltpu.VMEM)
    return pl.pallas_call(
        pack_kernel,
        in_specs=[pl.BlockSpec(memory_space=pltpu.SMEM), vmem, vmem, vmem],
        out_specs=vmem,
        out_shape=jax.ShapeDtypeStruct((samples, SLOTS + 16, targets.shape[1]), BF16),
        compiler_params=pltpu.CompilerParams(vmem_limit_bytes=16 * MIB),
        name="pack_rows",
    )(timesteps, owners, places, targets)


def weight_kernel(scale_ref, shift_ref, own_ref, other_ref, out_ref, bias_ref):
    parts, _, width = own_ref.shape
    gain = 1.0 + scale_ref[...]
    shift = jnp.broadcast_to(shift_ref[...], (8, shift_ref.shape[1]))
    high = shift.astype(BF16)
    low = (shift - high.astype(F32)).astype(BF16)
    for part in range(2 * parts):
        weight = own_ref[part] if part < parts else other_ref[part - parts]
        span = slice(part * width, (part + 1) * width)
        out_ref[:, span] = (gain * weight.astype(F32)).astype(BF16)
        total = jnp.dot(high, weight, preferred_element_type=F32)
        total += jnp.dot(low, weight, preferred_element_type=F32)
        bias_ref[:, span] = total[:1]


def fold_weight(scale, shift, own, other):
    parts, dmodel, width = own.shape
    vmem = pl.BlockSpec(memory_space=pltpu.VMEM)
    return pl.pallas_call(
        weight_kernel,
        in_specs=[vmem] * 4,
        out_specs=[vmem] * 2,
        out_shape=[
            jax.ShapeDtypeStruct((dmodel, 2 * parts * width), BF16),
            jax.ShapeDtypeStruct((1, 2 * parts * width), F32),
        ],
        compiler_params=pltpu.CompilerParams(vmem_limit_bytes=20 * MIB),
        name="fold_weight",
    )(scale.reshape(dmodel, 1), shift.reshape(1, dmodel), own, other)


def project_kernel(count, *refs):
    weight_ref, bias_ref, column_ref, spot_ref, other_spot_ref, got_ref = refs[:6]
    token_refs, (pair_ref, send_ref, query_ref) = refs[6 : 6 + count], refs[6 + count :]
    width = query_ref.shape[1]
    base = 0
    total = jnp.zeros(query_ref.shape, F32)
    for token_ref in token_refs:
        here = slice(base, base + token_ref.shape[0])
        base += token_ref.shape[0]
        qkv = jnp.dot(token_ref[...], weight_ref[...], preferred_element_type=F32) + bias_ref[...]
        qkv = qkv.astype(BF16)
        pair_ref[here, :] = qkv[:, width : 3 * width]
        send_ref[here, :] = qkv[:, 3 * width :]
        pick = onehot(column_ref[...] == spot_ref[:, here])
        total += jnp.dot(pick, qkv[:, :width], preferred_element_type=F32)
    pick = onehot(column_ref[...] == other_spot_ref[...])
    total += jnp.dot(pick, got_ref[:, :width], preferred_element_type=F32)
    query_ref[...] = total.astype(BF16)


def first_kernel(count, *refs):
    weight_ref, bias_ref, column_ref, spot_ref = refs[:4]
    token_refs, (pair_ref, send_ref, query_ref) = refs[4 : 4 + count], refs[4 + count :]
    width = query_ref.shape[1]
    base = 0
    total = jnp.zeros(query_ref.shape, F32)
    for token_ref in token_refs:
        here = slice(base, base + token_ref.shape[0])
        base += token_ref.shape[0]
        qkv = jnp.dot(token_ref[...], weight_ref[...], preferred_element_type=F32) + bias_ref[...]
        qkv = qkv.astype(BF16)
        pair_ref[here, :] = qkv[:, width : 3 * width]
        send_ref[here, :] = qkv[:, 3 * width :]
        pick = onehot(column_ref[...] == spot_ref[:, here])
        total += jnp.dot(pick, qkv[:, :width], preferred_element_type=F32)
    query_ref[...] = total.astype(BF16)


def project(weight, bias, column, spots, tokens, received=()):
    rows = sum(block.shape[0] for block in tokens)
    width = weight.shape[1] // 6
    vmem = pl.BlockSpec(memory_space=pltpu.VMEM)
    body = project_kernel if received else first_kernel
    return pl.pallas_call(
        functools.partial(body, len(tokens)),
        in_specs=[vmem] * (4 + len(received) + len(tokens)),
        out_specs=[vmem] * 3,
        out_shape=[
            jax.ShapeDtypeStruct((rows, 2 * width), BF16),
            jax.ShapeDtypeStruct((rows, 3 * width), BF16),
            jax.ShapeDtypeStruct((column.shape[0], width), BF16),
        ],
        compiler_params=pltpu.CompilerParams(vmem_limit_bytes=20 * MIB),
        cost_estimate=pl.CostEstimate(
            flops=4 * rows * weight.size, bytes_accessed=8 * MIB, transcendentals=0
        ),
        name="project",
    )(weight, bias, column, spots, *received, *tokens)


def attend_kernel(count, column_ref, row_ref, spot_ref, target_ref, *refs):
    pair_refs, got_refs, query_refs = refs[:count], refs[count : 2 * count], refs[2 * count : 3 * count]
    out_ref, key_ref, first_ref, second_ref, query_ref, diff_ref = refs[3 * count :]
    slots, width = query_ref.shape
    length = key_ref.shape[0]
    base = 0
    for block_ref in (*pair_refs, *got_refs):
        here = slice(base, base + block_ref.shape[0])
        base += block_ref.shape[0]
        skip = block_ref.shape[1] - 2 * width
        value = block_ref[:, skip + width :]
        left = lax.broadcasted_iota(jnp.int32, value.shape, 1) < HEAD_DIM
        one = jnp.ones(value.shape, BF16)
        key_ref[here, :] = block_ref[:, skip : skip + width]
        first_ref[here, :] = jnp.where(left, value, one)
        second_ref[here, :] = jnp.where(left, one, value)
    query = sum(part[...].astype(F32) for part in query_refs)
    pick = onehot(column_ref[...] == spot_ref[...])
    query += jnp.dot(pick, got_refs[-1][:, :width], preferred_element_type=F32)
    query_ref[...] = query
    factor = math.log2(math.e) / math.sqrt(HEAD_DIM)
    part = 256
    half = lax.broadcasted_iota(jnp.int32, (part, width), 1) < HEAD_DIM
    for start in range(0, slots, part):
        query = query_ref[start : start + part, :]
        outs = []
        for mask, value_ref in ((half, first_ref), (~half, second_ref)):
            mine = jnp.where(mask, query, 0.0).astype(BF16)
            scores = lax.dot_general(
                mine, key_ref[...], (((1,), (1,)), ((), ())), preferred_element_type=F32
            )
            top = jnp.max(scores, axis=1, keepdims=True)
            probs = jnp.exp2((scores - top) * factor).astype(BF16)
            mixed = jnp.dot(probs, value_ref[...], preferred_element_type=F32)
            outs.append(mixed / pltpu.roll(mixed, HEAD_DIM, 1))
        attended = jnp.where(half, outs[0], outs[1])
        target = target_ref[start : start + part, :].astype(F32)
        diff_ref[start : start + part, :] = (attended - target).astype(BF16)
    for start in range(0, length, part):
        spots = lax.broadcasted_iota(jnp.int32, (part, slots), 0) + start
        spread = onehot(row_ref[...] == spots)
        out_ref[start : start + part, :] = jnp.dot(
            spread, diff_ref[...], preferred_element_type=F32
        ).astype(BF16)


def attend(column, row, spots, targets, pairs, received, queries):
    slots, width = targets.shape
    length = sum(block.shape[0] for block in (*pairs, *received))
    vmem = pl.BlockSpec(memory_space=pltpu.VMEM)
    return pl.pallas_call(
        functools.partial(attend_kernel, len(pairs)),
        in_specs=[vmem] * (4 + 3 * len(pairs)),
        out_specs=vmem,
        out_shape=jax.ShapeDtypeStruct((length, width), BF16),
        scratch_shapes=[
            pltpu.VMEM((length, width), BF16),
            pltpu.VMEM((length, width), BF16),
            pltpu.VMEM((length, width), BF16),
            pltpu.VMEM((slots, width), F32),
            pltpu.VMEM((slots, width), BF16),
        ],
        compiler_params=pltpu.CompilerParams(vmem_limit_bytes=28 * MIB),
        name="attend",
    )(column, row, spots, targets, *pairs, *received, *queries)


def after(array, *earlier):
    return lax.optimization_barrier((array, earlier))[0]


def shards(
    latents, noise, timesteps, time_weight, qkv_weight, cached_targets, cache_owner, cache_pos
):
    dmodel = latents.shape[2]
    own = latents.shape[1]
    width = qkv_weight.shape[2]
    samples = lax.axis_size("fsdp")
    group = lax.axis_size("seq")
    crows = cached_targets.shape[0]
    me = lax.axis_index("seq")
    swap = [(i, i ^ 1) for i in range(group)]
    onward = [(i, (i + 2 - 4 * (i % 2)) % group) for i in range(group)]
    backward = [(i, (i - 2 + 4 * (i % 2)) % group) for i in range(group)]

    def spots_of(device, hop):
        origin = jnp.where(device % 2 == 0, device - 2 * hop, device + 2 * hop) % group
        return own * origin + jnp.arange(own, dtype=jnp.int32)

    def group_spots(device, hop_list):
        return jnp.concatenate([spots_of(device, hop) for hop in hop_list])[None, :]

    normed = normalize(timesteps, latents[0], noise[0])
    up1 = lax.ppermute(normed, "seq", onward)
    down1 = lax.ppermute(normed, "seq", backward)
    sent = pack_rows(
        timesteps, cache_owner.reshape(1, crows), cache_pos.reshape(1, crows), cached_targets, samples
    )
    got = lax.all_to_all(after(sent, normed), "fsdp", 0, 0, tiled=True)
    raw = qkv_weight.transpose(1, 0, 2)
    other_raw = lax.ppermute(after(raw, normed), "seq", swap)
    up2 = lax.ppermute(up1, "seq", onward)
    down2 = lax.ppermute(down1, "seq", backward)

    targets = got[:, :SLOTS].reshape(samples * SLOTS, width)
    extra = got[:, SLOTS].astype(F32)
    high, low = extra[:, :SLOTS], extra[:, SLOTS : 2 * SLOTS]
    places = jnp.where(high > 0.5, (high - 1.0) * 64.0 + low, -1.0).astype(jnp.int32)
    column = places.reshape(samples * SLOTS, 1)
    row = places.reshape(1, samples * SLOTS)
    stamps = (extra[:, 2 * SLOTS] * 32.0 + extra[:, 2 * SLOTS + 1]).astype(jnp.int32)
    part = jnp.dot(embed_times(stamps), time_weight, preferred_element_type=F32)
    up3 = lax.ppermute(up2, "seq", onward)
    modulation = lax.all_to_all(after(part, up1), "fsdp", 0, 0, tiled=True).reshape(2 * dmodel)
    down3 = lax.ppermute(after(down2, part), "seq", backward)
    weight, bias = fold_weight(modulation[dmodel:], modulation[:dmodel], raw, other_raw)

    hops = ([0, 1, -1, 2, -2], [3, -3], [4])
    spots = [group_spots(me, hop_list) for hop_list in hops]
    other_spots = [group_spots(me ^ 1, hop_list) for hop_list in hops]
    first = project(weight, bias, column, spots[0], [normed, up1, down1, up2, down2])
    got_first = lax.ppermute(first[1], "seq", swap)
    up4 = lax.ppermute(after(up3, *first), "seq", onward)
    second = project(
        weight, bias, column, spots[1], [up3, down3], (other_spots[0], got_first)
    )
    got_second = lax.ppermute(second[1], "seq", swap)
    third = project(weight, bias, column, spots[2], [up4], (other_spots[1], got_second))
    got_third = lax.ppermute(third[1], "seq", swap)
    pairs, _, queries = zip(first, second, third)
    received = (got_first, got_second, got_third)
    return attend(column, row, other_spots[2], targets, pairs, received, queries)[None]


def solution(mesh):
    placed = (
        P("fsdp", "seq", None),
        P("fsdp", "seq", None),
        P("fsdp"),
        P(None, "fsdp"),
        P(None, None, "seq"),
        P("fsdp", "seq"),
        P("fsdp", None),
        P("fsdp"),
    )
    return jax.shard_map(
        shards, mesh=mesh, in_specs=placed, out_specs=P("fsdp", None, "seq"), check_vma=False
    )
```

time: 111 us -> 106 us (0.955)
  starting transfers between devices: 15.7 us -> 57.7 us
  waiting for transfers between devices: 41.6 us -> 13.9 us
  between operations: 14.3 us -> 1.61 us
  other arithmetic: 5.71 us -> 0.56 us
  matrix products: 2.45 us -> 0.15 us
  Pallas kernels: 23.1 us -> 24.7 us
    ppermute x0 -> x11, starting transfers between devices: none -> 42.9 us  [the longest x1 11.5 us: shards(): up1 = lax.ppermute(normed, 'seq', onward)]
    all_gather x1 -> x0, waiting for transfers between devices: 25.5 us -> none  [shards(): tokens = lax.all_gather(normed, 'seq', axis=0, tiled=True)]
    pallas_call x1 -> x6, Pallas kernels: 19.2 us -> 24 us  [the longest x3 10.3 us: project(): pl.pallas_call(functools.partial(body, len(tokens)), in_specs=[vmem] * (4...]
    all_to_all x2, waiting for transfers between devices: 16 us -> 12.5 us  [the longest x1 8.01 us: shards(): lax.all_to_all(after(part, up1), 'fsdp', 0, 0, tiled=True)]
    pallas_call x1, Pallas kernels: 3.87 us -> 0.64 us  [normalize(): pl.pallas_call(norm_kernel, grid=(rows // block,), in_specs=[pl.BlockSpec...]
    convert_element_type x4 -> x1, other arithmetic: 3.19 us -> 0.01 us  [shards(): extra = got[:, SLOTS].astype(F32)]
    convert_element_type x1 -> x0, local copies, waits for them, and re-layouts: 2.81 us -> none  [shards(): flat_weight = qkv_weight.reshape(dmodel, 3 * width).astype(F32)]
    dot_general x3 -> x0, matrix products: 2.31 us -> none  [the longest x1 1.03 us: pack_rows(): before = jnp.dot(strict, owned.astype(BF16), preferred_element_type=F32)]
  transfers between devices with their start and end apart: 3 -> 13, of which waited for: 3 -> 4; matrix products, arithmetic and copies ran while one was open for 14% -> 3% of each run, Pallas kernels for 0% -> 14%
where the time goes in v2:
time: 106 us
  starting transfers between devices  57.7 us (54%)
  Pallas kernels  24.7 us (23%)
  waiting for transfers between devices  13.9 us (13%)
  local copies, waits for them, and re-layouts  7.05 us (7%)
  between operations  1.61 us (2%)
    ppermute x1, starting transfers between devices, shards(): up1 = lax.ppermute(normed, 'seq', onward)  11.5 us
    pallas_call x3, Pallas kernels, project(): pl.pallas_call(functools.partial(body, len(tokens)), in_specs=[vmem] * (4...  10.3 us
    all_to_all x1, starting transfers between devices, shards(): got = lax.all_to_all(after(sent, normed), 'fsdp', 0, 0, tiled=True)  9.67 us
    pallas_call x1, Pallas kernels, attend(): pl.pallas_call(functools.partial(attend_kernel, len(pairs)), in_specs=[vm...  8.56 us
    all_to_all x1, waiting for transfers between devices, shards(): lax.all_to_all(after(part, up1), 'fsdp', 0, 0, tiled=True)  8.01 us
    ppermute x1, starting transfers between devices, shards(): got_first = lax.ppermute(first[1], 'seq', swap)  5.07 us
    all_to_all x1, starting transfers between devices, shards(): lax.all_to_all(after(part, up1), 'fsdp', 0, 0, tiled=True)  5.07 us
    ppermute x1, starting transfers between devices, shards(): up4 = lax.ppermute(after(up3, *first), 'seq', onward)  4.85 us
  transfers between devices with their start and end apart: 13, of which 4 were waited for; matrix products, arithmetic and copies ran while one was open for 3% of the time, Pallas kernels for 14%

profile of v2, /device:TPU:1, one launch (start us, length us, event | category | flops | bytes accessed | tf_op | source)
XLA Modules:
  0.0 105.6 jit_solution(17294147993683061810)
XLA Ops:
  0.7 1.1 %copy-done.3 = bf16[1,128,2432]{2,1,0:T(8,128)(2,1)S(1)} copy-done((bf16[1,128,2432]{2,1,0:T(8,128)(2,1)S(1)}, bf16[1,128,2432]{2,1,0:T(8,128)(2,1)}, u32[]{:S(2)}) %copy-start.3) | copy-done | bytes 622616
  1.8 1.1 %copy-done.4 = bf16[1,128,2432]{2,1,0:T(8,128)(2,1)S(1)} copy-done((bf16[1,128,2432]{2,1,0:T(8,128)(2,1)S(1)}, bf16[1,128,2432]{2,1,0:T(8,128)(2,1)}, u32[]{:S(2)}) %copy-start.4) | copy-done | bytes 622616
  2.8 0.6 normalize.1.refs_4_
  3.5 11.5 %collective-permute-start = (bf16[128,2432]{1,0:T(8,128)(2,1)S(1)}, bf16[128,2432]{1,0:T(8,128)(2,1)S(1)}, u32[]{:S(2)}, u32[]{:S(2)}) collective-permute-start(bf16[128,2432]{1,0:T(8,128)(2,1)S(1)} %normalize.1.refs_4_), channel_id=1, source_target_pairs={{0,64},{32,480},{64,128},{96,32},{128,192},{160,96},{192,256},{224... | collective-permute-start | bytes 1867784 | tf_op jit(solution)/shard_map/ppermute | solution.py:281
  15.0 1.9 %collective-permute-start.2 = (bf16[128,2432]{1,0:T(8,128)(2,1)S(1)}, bf16[128,2432]{1,0:T(8,128)(2,1)}, u32[]{:S(2)}, u32[]{:S(2)}) collective-permute-start(bf16[128,2432]{1,0:T(8,128)(2,1)S(1)} %normalize.1.refs_4_), channel_id=1, source_target_pairs={{0,448},{32,96},{64,0},{96,160},{128,64},{160,224},{192,128},{224,... | collective-permute-start | bytes 1867784 | tf_op jit(solution)/shard_map/ppermute | solution.py:282
  17.0 1.5 %pack_rows.1 = bf16[32,48,128]{2,1,0:T(8,128)(2,1)} custom-call(s32[1]{0:T(128)S(6)} %copy.30.stamp_ref, s32[1,512]{1,0:T(1,128)S(1)} %bitcast.16, s32[1,512]{1,0:T(1,128)S(1)} %bitcast.17, bf16[512,128]{1,0:T(8,128)(2,1)S(1)} %copy-done.5), custom_call_target="tpu_custom_call" | custom-call | tf_op jit(solution)/shard_map/pack_rows/pallas_call | solution.py:87
  18.4 9.7 %all-to-all-start = ((bf16[32,48,128]{2,1,0:T(8,128)(2,1)}), bf16[32,48,128]{2,1,0:T(8,128)(2,1)S(1)}, u32[]{:S(2)}, u32[]{:S(2)}) async-start(bf16[32,48,128]{2,1,0:T(8,128)(2,1)} %pack_rows.1), calls=%async_computation | async-start | bytes 786432 | tf_op jit(solution)/shard_map/all_to_all | solution.py:286
  28.1 3.1 %collective-permute-start.1 = (bf16[3,2432,128]{2,1,0:T(8,128)(2,1)}, bf16[3,2432,128]{2,1,0:T(8,128)(2,1)}, u32[]{:S(2)}, u32[]{:S(2)}) collective-permute-start(bf16[3,2432,128]{2,1,0:T(8,128)(2,1)} %bitcast.7.own_ref), channel_id=1, source_target_pairs={{0,32},{32,0},{64,96},{96,64},{128,160},{160,128},{192,224},{224,1... | collective-permute-start | bytes 5603336 | tf_op jit(solution)/shard_map/ppermute | solution.py:288
  31.7 0.0 collective-permute-done.refs_5_
  31.7 3.6 %collective-permute-start.3 = (bf16[128,2432]{1,0:T(8,128)(2,1)S(1)}, bf16[128,2432]{1,0:T(8,128)(2,1)}, u32[]{:S(2)}, u32[]{:S(2)}) collective-permute-start(bf16[128,2432]{1,0:T(8,128)(2,1)S(1)} %collective-permute-done.refs_5_), channel_id=1, source_target_pairs={{0,64},{32,480},{64,128},{96,32},{128,192},{160,96},{192,256},{224... | collective-permute-start | bytes 1867784 | tf_op jit(solution)/shard_map/ppermute | solution.py:289
  35.3 0.0 collective-permute-done.2.refs_6_
  35.4 1.9 %collective-permute-start.4 = (bf16[128,2432]{1,0:T(8,128)(2,1)}, bf16[128,2432]{1,0:T(8,128)(2,1)}, u32[]{:S(2)}, u32[]{:S(2)}) collective-permute-start(bf16[128,2432]{1,0:T(8,128)(2,1)} %collective-permute-done.2.refs_6_), channel_id=1, source_target_pairs={{0,448},{32,96},{64,0},{96,160},{128,64},{160,224},{192,128},{224,... | collective-permute-start | bytes 1867784 | tf_op jit(solution)/shard_map/ppermute | solution.py:290
  37.3 4.5 %all-to-all-done = bf16[32,48,128]{2,1,0:T(8,128)(2,1)S(1)} async-done(((bf16[32,48,128]{2,1,0:T(8,128)(2,1)}), bf16[32,48,128]{2,1,0:T(8,128)(2,1)S(1)}, u32[]{:S(2)}, u32[]{:S(2)}) %all-to-all-start) | async-done | bytes 393248 | tf_op jit(solution)/shard_map/all_to_all | solution.py:286
  41.8 0.2 fusion.3
  42.0 0.1 multiply_cosine_fusion
  42.2 0.1 fusion
  42.3 0.7 copy.14
  43.0 5.1 %all-to-all-start.1 = ((f32[32,1,152]{2,1,0:T(1,128)}), f32[32,1,152]{2,1,0:T(1,128)S(1)}, u32[]{:S(2)}, u32[]{:S(2)}) async-start(f32[32,1,152]{2,1,0:T(1,128)} %copy.14), calls=%async_computation.1 | async-start | bytes 65536 | tf_op jit(solution)/shard_map/all_to_all | solution.py:301
  48.1 0.1 fusion.5
  48.1 0.5 reshape.62.refs_2_.column_ref
  48.7 8.0 %all-to-all-done.1 = f32[32,1,152]{2,1,0:T(1,128)S(1)} async-done(((f32[32,1,152]{2,1,0:T(1,128)}), f32[32,1,152]{2,1,0:T(1,128)S(1)}, u32[]{:S(2)}, u32[]{:S(2)}) %all-to-all-start.1) | async-done | bytes 19488 | tf_op jit(solution)/shard_map/all_to_all | solution.py:301
  56.7 0.1 slice_reduce_fusion
  56.8 0.4 reshape.61.scale_ref
  57.2 0.1 reshape.59.shift_ref
  57.3 0.0 collective-permute-done.4.refs_8_
  57.3 1.9 %collective-permute-start.7 = (bf16[128,2432]{1,0:T(8,128)(2,1)}, bf16[128,2432]{1,0:T(8,128)(2,1)}, u32[]{:S(2)}, u32[]{:S(2)}) collective-permute-start(bf16[128,2432]{1,0:T(8,128)(2,1)} %collective-permute-done.4.refs_8_), channel_id=1, source_target_pairs={{0,448},{32,96},{64,0},{96,160},{128,64},{160,224},{192,128},{224,... | collective-permute-start | bytes 1867784 | tf_op jit(solution)/shard_map/ppermute | solution.py:302
  59.2 0.0 collective-permute-done.3.refs_7_
  59.2 4.7 %collective-permute-start.6 = (bf16[128,2432]{1,0:T(8,128)(2,1)}, bf16[128,2432]{1,0:T(8,128)(2,1)}, u32[]{:S(2)}, u32[]{:S(2)}) collective-permute-start(bf16[128,2432]{1,0:T(8,128)(2,1)} %collective-permute-done.3.refs_7_), channel_id=1, source_target_pairs={{0,64},{32,480},{64,128},{96,32},{128,192},{160,96},{192,256},{224... | collective-permute-start | bytes 1867784 | tf_op jit(solution)/shard_map/ppermute | solution.py:300
  63.9 0.0 collective-permute-done.1.other_ref
  63.9 3.7 %fold_weight.1 = (bf16[2432,768]{1,0:T(8,128)(2,1)S(1)}, f32[1,768]{1,0:T(1,128)S(1)}) custom-call(f32[2432,1]{1,0:T(8,128)S(1)} %reshape.61.scale_ref, f32[1,2432]{1,0:T(1,128)S(1)} %reshape.59.shift_ref, bf16[3,2432,128]{2,1,0:T(8,128)(2,1)} %bitcast.7.own_ref, bf16[3,2432,128]{2,1,0:T(8,128)(2,1)} %collective-permute-done.1.other_ref), custom_call_target="tpu_custom_call" | custom-call | tf_op jit(solution)/shard_map/fold_weight/pallas_call | solution.py:115
  67.6 0.0 copy-done.9
  67.6 6.4 %project.3 = (bf16[640,256]{1,0:T(8,128)(2,1)S(1)}, bf16[640,384]{1,0:T(8,128)(2,1)S(1)}, bf16[1024,128]{1,0:T(8,128)(2,1)S(1)}) custom-call(bf16[2432,768]{1,0:T(8,128)(2,1)S(1)} %get-tuple-element.24.refs_0_, f32[1,768]{1,0:T(1,128)S(1)} %get-tuple-element.25.refs_1_, s32[1024,1]{1,0:T(8,128)S(1)} %reshape.62.refs_2_.column_ref, ...), custom_call_target="tpu_custom_call" | custom-call | flops 4781506560 | bytes 8388608 | tf_op jit(solution)/shard_map/project/pallas_call | solution.py:171
  74.1 5.1 %collective-permute-start.5 = (bf16[640,384]{1,0:T(8,128)(2,1)S(1)}, bf16[640,384]{1,0:T(8,128)(2,1)S(1)}, u32[]{:S(2)}, u32[]{:S(2)}) collective-permute-start(bf16[640,384]{1,0:T(8,128)(2,1)S(1)} %get-tuple-element.27), channel_id=1, source_target_pairs={{0,32},{32,0},{64,96},{96,64},{128,160},{160,128},{192,224},{224,1... | collective-permute-start | bytes 1474568 | tf_op jit(solution)/shard_map/ppermute | solution.py:309
  79.4 0.0 collective-permute-done.6.refs_6_
  79.4 4.9 %collective-permute-start.9 = (bf16[128,2432]{1,0:T(8,128)(2,1)}, bf16[128,2432]{1,0:T(8,128)(2,1)S(1)}, u32[]{:S(2)}, u32[]{:S(2)}) collective-permute-start(bf16[128,2432]{1,0:T(8,128)(2,1)} %collective-permute-done.6.refs_6_), channel_id=1, source_target_pairs={{0,64},{32,480},{64,128},{96,32},{128,192},{160,96},{192,256},{224... | collective-permute-start | bytes 1867784 | tf_op jit(solution)/shard_map/ppermute | solution.py:310
  84.3 0.0 collective-permute-done.7.refs_7_
  84.3 0.0 collective-permute-done.5.refs_5_.refs_3_
  84.3 2.0 %copy-done.2 = bf16[2432,768]{1,0:T(8,128)(2,1)S(1)} copy-done((bf16[2432,768]{1,0:T(8,128)(2,1)S(1)}, bf16[2432,768]{1,0:T(8,128)(2,1)}, u32[]{:S(2)}) %copy-start.2) | copy-done | bytes 3735576
  86.4 3.0 %project.4 = (bf16[256,256]{1,0:T(8,128)(2,1)S(1)}, bf16[256,384]{1,0:T(8,128)(2,1)S(1)}, bf16[1024,128]{1,0:T(8,128)(2,1)S(1)}) custom-call(bf16[2432,768]{1,0:T(8,128)(2,1)S(1)} %copy-done.2, f32[1,768]{1,0:T(1,128)S(1)} %get-tuple-element.25.refs_1_, s32[1024,1]{1,0:T(8,128)S(1)} %reshape.62.refs_2_.column_ref, s32[1,256]{1,0:T(1,128)S(1)} %bitcast.18, ...), custom_call_target="tpu_custom_call" | custom-call | flops 1912602624 | bytes 8388608 | tf_op jit(solution)/shard_map/project/pallas_call | solution.py:171
  89.4 1.9 %collective-permute-start.8 = (bf16[256,384]{1,0:T(8,128)(2,1)S(1)}, bf16[256,384]{1,0:T(8,128)(2,1)S(1)}, u32[]{:S(2)}, u32[]{:S(2)}) collective-permute-start(bf16[256,384]{1,0:T(8,128)(2,1)S(1)} %get-tuple-element.30), channel_id=1, source_target_pairs={{0,32},{32,0},{64,96},{96,64},{128,160},{160,128},{192,224},{224,1... | collective-permute-start | bytes 589832 | tf_op jit(solution)/shard_map/ppermute | solution.py:314
  91.3 0.4 collective-permute-done.9.refs_6_
  91.7 1.0 collective-permute-done.8.refs_5_.refs_4_
  92.7 0.9 project.5
  93.6 2.4 %collective-permute-start.10 = (bf16[128,384]{1,0:T(8,128)(2,1)S(1)}, bf16[128,384]{1,0:T(8,128)(2,1)S(1)}, u32[]{:S(2)}, u32[]{:S(2)}) collective-permute-start(bf16[128,384]{1,0:T(8,128)(2,1)S(1)} %get-tuple-element.34), channel_id=1, source_target_pairs={{0,32},{32,0},{64,96},{96,64},{128,160},{160,128},{192,224},{224,1... | collective-permute-start | bytes 294920 | tf_op jit(solution)/shard_map/ppermute | solution.py:316
  96.0 0.1 reshape.56.row_ref
  96.1 1.0 slice.39
  97.1 0.0 collective-permute-done.10.refs_5_
  97.1 8.6 %attend.1 = bf16[2048,128]{1,0:T(8,128)(2,1)} custom-call(s32[1024,1]{1,0:T(8,128)S(1)} %reshape.62.refs_2_.column_ref, s32[1,1024]{1,0:T(1,128)S(1)} %reshape.56.row_ref, s32[1,128]{1,0:T(1,128)S(1)} %iota_add_fusion.5.spot_ref, bf16[1024,128]{1,0:T(8,128)(2,1)S(1)} %bitcast.12, bf16[640,256]{1,0:T(8,128)(2,1)S(1)} %get-tuple-element.26.refs_0_, ...), custom_call_target="tpu_custom_call" | custom-call | tf_op jit(solution)/shard_map/attend/pallas_call | solution.py:238
  (40 shorter events, 0.2 us)
Async XLA Ops:
  0.0 42.2 %copy-start = (bf16[256,152]{0,1:T(8,128)(2,1)S(1)}, bf16[256,152]{0,1:T(8,128)(2,1)}, u32[]{:S(2)}) copy-start(bf16[256,152]{0,1:T(8,128)(2,1)} %param.11) | copy-start | bytes 233476
  0.0 16.9 %copy-start.6 = (s32[512,1]{0,1:T(1,128)S(1)}, s32[512,1]{0,1:T(1,128)}, u32[]{:S(2)}) copy-start(s32[512,1]{0,1:T(1,128)} %param.14) | copy-start | bytes 6148
  0.0 16.9 %copy-start.7 = (s32[512]{0:T(512)S(1)}, s32[512]{0:T(512)}, u32[]{:S(2)}) copy-start(s32[512]{0:T(512)} %param.15) | copy-start | bytes 6148
  0.7 1.1 %copy-start.3 = (bf16[1,128,2432]{2,1,0:T(8,128)(2,1)S(1)}, bf16[1,128,2432]{2,1,0:T(8,128)(2,1)}, u32[]{:S(2)}) copy-start(bf16[1,128,2432]{2,1,0:T(8,128)(2,1)} %param.8) | copy-start | bytes 1867780
  1.8 1.1 %copy-start.4 = (bf16[1,128,2432]{2,1,0:T(8,128)(2,1)S(1)}, bf16[1,128,2432]{2,1,0:T(8,128)(2,1)}, u32[]{:S(2)}) copy-start(bf16[1,128,2432]{2,1,0:T(8,128)(2,1)} %param.9) | copy-start | bytes 1867780
  2.8 14.1 %copy-start.5 = (bf16[512,128]{1,0:T(8,128)(2,1)S(1)}, bf16[512,128]{1,0:T(8,128)(2,1)}, u32[]{:S(2)}) copy-start(bf16[512,128]{1,0:T(8,128)(2,1)} %target_ref.1) | copy-start | bytes 393220
  3.5 28.2 %collective-permute-start = (bf16[128,2432]{1,0:T(8,128)(2,1)S(1)}, bf16[128,2432]{1,0:T(8,128)(2,1)S(1)}, u32[]{:S(2)}, u32[]{:S(2)}) collective-permute-start(bf16[128,2432]{1,0:T(8,128)(2,1)S(1)} %normalize.1.refs_4_), channel_id=1, source_target_pairs={{0,64},{32,480},{64,128},{96,32},{128,192},{160,96},{192,256},{224... | collective-permute-start | bytes 1867784 | tf_op jit(solution)/shard_map/ppermute | solution.py:281
  15.0 20.3 %collective-permute-start.2 = (bf16[128,2432]{1,0:T(8,128)(2,1)S(1)}, bf16[128,2432]{1,0:T(8,128)(2,1)}, u32[]{:S(2)}, u32[]{:S(2)}) collective-permute-start(bf16[128,2432]{1,0:T(8,128)(2,1)S(1)} %normalize.1.refs_4_), channel_id=1, source_target_pairs={{0,448},{32,96},{64,0},{96,160},{128,64},{160,224},{192,128},{224,... | collective-permute-start | bytes 1867784 | tf_op jit(solution)/shard_map/ppermute | solution.py:282
  18.4 23.4 %all-to-all-start = ((bf16[32,48,128]{2,1,0:T(8,128)(2,1)}), bf16[32,48,128]{2,1,0:T(8,128)(2,1)S(1)}, u32[]{:S(2)}, u32[]{:S(2)}) async-start(bf16[32,48,128]{2,1,0:T(8,128)(2,1)} %pack_rows.1), calls=%async_computation | async-start | bytes 786432 | tf_op jit(solution)/shard_map/all_to_all | solution.py:286
  28.1 35.8 %collective-permute-start.1 = (bf16[3,2432,128]{2,1,0:T(8,128)(2,1)}, bf16[3,2432,128]{2,1,0:T(8,128)(2,1)}, u32[]{:S(2)}, u32[]{:S(2)}) collective-permute-start(bf16[3,2432,128]{2,1,0:T(8,128)(2,1)} %bitcast.7.own_ref), channel_id=1, source_target_pairs={{0,32},{32,0},{64,96},{96,64},{128,160},{160,128},{192,224},{224,1... | collective-permute-start | bytes 5603336 | tf_op jit(solution)/shard_map/ppermute | solution.py:288
  31.7 32.2 %copy-start.8 = (bf16[128,2432]{1,0:T(8,128)(2,1)}, bf16[128,2432]{1,0:T(8,128)(2,1)S(1)}, u32[]{:S(2)}) copy-start(bf16[128,2432]{1,0:T(8,128)(2,1)S(1)} %collective-permute-done.refs_5_) | copy-start | bytes 1867780
  31.7 27.5 %collective-permute-start.3 = (bf16[128,2432]{1,0:T(8,128)(2,1)S(1)}, bf16[128,2432]{1,0:T(8,128)(2,1)}, u32[]{:S(2)}, u32[]{:S(2)}) collective-permute-start(bf16[128,2432]{1,0:T(8,128)(2,1)S(1)} %collective-permute-done.refs_5_), channel_id=1, source_target_pairs={{0,64},{32,480},{64,128},{96,32},{128,192},{160,96},{192,256},{224... | collective-permute-start | bytes 1867784 | tf_op jit(solution)/shard_map/ppermute | solution.py:289
  35.4 21.9 %collective-permute-start.4 = (bf16[128,2432]{1,0:T(8,128)(2,1)}, bf16[128,2432]{1,0:T(8,128)(2,1)}, u32[]{:S(2)}, u32[]{:S(2)}) collective-permute-start(bf16[128,2432]{1,0:T(8,128)(2,1)} %collective-permute-done.2.refs_6_), channel_id=1, source_target_pairs={{0,448},{32,96},{64,0},{96,160},{128,64},{160,224},{192,128},{224,... | collective-permute-start | bytes 1867784 | tf_op jit(solution)/shard_map/ppermute | solution.py:290
  41.8 15.0 %copy-start.10 = (bf16[32,48,128]{2,1,0:T(8,128)(2,1)}, bf16[32,48,128]{2,1,0:T(8,128)(2,1)S(1)}, u32[]{:S(2)}) copy-start(bf16[32,48,128]{2,1,0:T(8,128)(2,1)S(1)} %all-to-all-done) | copy-start | bytes 1179652
  43.0 13.7 %all-to-all-start.1 = ((f32[32,1,152]{2,1,0:T(1,128)}), f32[32,1,152]{2,1,0:T(1,128)S(1)}, u32[]{:S(2)}, u32[]{:S(2)}) async-start(f32[32,1,152]{2,1,0:T(1,128)} %copy.14), calls=%async_computation.1 | async-start | bytes 65536 | tf_op jit(solution)/shard_map/all_to_all | solution.py:301
  57.3 27.0 %collective-permute-start.7 = (bf16[128,2432]{1,0:T(8,128)(2,1)}, bf16[128,2432]{1,0:T(8,128)(2,1)}, u32[]{:S(2)}, u32[]{:S(2)}) collective-permute-start(bf16[128,2432]{1,0:T(8,128)(2,1)} %collective-permute-done.4.refs_8_), channel_id=1, source_target_pairs={{0,448},{32,96},{64,0},{96,160},{128,64},{160,224},{192,128},{224,... | collective-permute-start | bytes 1867784 | tf_op jit(solution)/shard_map/ppermute | solution.py:302
  59.2 20.2 %collective-permute-start.6 = (bf16[128,2432]{1,0:T(8,128)(2,1)}, bf16[128,2432]{1,0:T(8,128)(2,1)}, u32[]{:S(2)}, u32[]{:S(2)}) collective-permute-start(bf16[128,2432]{1,0:T(8,128)(2,1)} %collective-permute-done.3.refs_7_), channel_id=1, source_target_pairs={{0,64},{32,480},{64,128},{96,32},{128,192},{160,96},{192,256},{224... | collective-permute-start | bytes 1867784 | tf_op jit(solution)/shard_map/ppermute | solution.py:300
  63.9 3.7 %copy-start.9 = (bf16[128,2432]{1,0:T(8,128)(2,1)S(1)}, bf16[128,2432]{1,0:T(8,128)(2,1)}, u32[]{:S(2)}) copy-start(bf16[128,2432]{1,0:T(8,128)(2,1)} %copy-done.8) | copy-start | bytes 1867780
  67.6 6.5 %copy-start.1 = (bf16[2432,768]{1,0:T(8,128)(2,1)}, bf16[2432,768]{1,0:T(8,128)(2,1)S(1)}, u32[]{:S(2)}) copy-start(bf16[2432,768]{1,0:T(8,128)(2,1)S(1)} %get-tuple-element.24.refs_0_) | copy-start | bytes 11206660
  74.1 10.2 %collective-permute-start.5 = (bf16[640,384]{1,0:T(8,128)(2,1)S(1)}, bf16[640,384]{1,0:T(8,128)(2,1)S(1)}, u32[]{:S(2)}, u32[]{:S(2)}) collective-permute-start(bf16[640,384]{1,0:T(8,128)(2,1)S(1)} %get-tuple-element.27), channel_id=1, source_target_pairs={{0,32},{32,0},{64,96},{96,64},{128,160},{160,128},{192,224},{224,1... | collective-permute-start | bytes 1474568 | tf_op jit(solution)/shard_map/ppermute | solution.py:309
  79.4 12.3 %collective-permute-start.9 = (bf16[128,2432]{1,0:T(8,128)(2,1)}, bf16[128,2432]{1,0:T(8,128)(2,1)S(1)}, u32[]{:S(2)}, u32[]{:S(2)}) collective-permute-start(bf16[128,2432]{1,0:T(8,128)(2,1)} %collective-permute-done.6.refs_6_), channel_id=1, source_target_pairs={{0,64},{32,480},{64,128},{96,32},{128,192},{160,96},{192,256},{224... | collective-permute-start | bytes 1867784 | tf_op jit(solution)/shard_map/ppermute | solution.py:310
  84.3 2.1 %copy-start.2 = (bf16[2432,768]{1,0:T(8,128)(2,1)S(1)}, bf16[2432,768]{1,0:T(8,128)(2,1)}, u32[]{:S(2)}) copy-start(bf16[2432,768]{1,0:T(8,128)(2,1)} %copy-done.1) | copy-start | bytes 11206660
  89.4 3.3 %collective-permute-start.8 = (bf16[256,384]{1,0:T(8,128)(2,1)S(1)}, bf16[256,384]{1,0:T(8,128)(2,1)S(1)}, u32[]{:S(2)}, u32[]{:S(2)}) collective-permute-start(bf16[256,384]{1,0:T(8,128)(2,1)S(1)} %get-tuple-element.30), channel_id=1, source_target_pairs={{0,32},{32,0},{64,96},{96,64},{128,160},{160,128},{192,224},{224,1... | collective-permute-start | bytes 589832 | tf_op jit(solution)/shard_map/ppermute | solution.py:314
  93.6 3.5 %collective-permute-start.10 = (bf16[128,384]{1,0:T(8,128)(2,1)S(1)}, bf16[128,384]{1,0:T(8,128)(2,1)S(1)}, u32[]{:S(2)}, u32[]{:S(2)}) collective-permute-start(bf16[128,384]{1,0:T(8,128)(2,1)S(1)} %get-tuple-element.34), channel_id=1, source_target_pairs={{0,32},{32,0},{64,96},{96,64},{128,160},{160,128},{192,224},{224,1... | collective-permute-start | bytes 294920 | tf_op jit(solution)/shard_map/ppermute | solution.py:316

commit v3 on v2

--- a/solution.py
+++ b/solution.py
@@ -100,13 +100,13 @@
     shift = jnp.broadcast_to(shift_ref[...], (8, shift_ref.shape[1]))
     high = shift.astype(BF16)
     low = (shift - high.astype(F32)).astype(BF16)
+    both = jnp.concatenate([high, low], axis=0)
     for part in range(2 * parts):
         weight = own_ref[part] if part < parts else other_ref[part - parts]
         span = slice(part * width, (part + 1) * width)
         out_ref[:, span] = (gain * weight.astype(F32)).astype(BF16)
-        total = jnp.dot(high, weight, preferred_element_type=F32)
-        total += jnp.dot(low, weight, preferred_element_type=F32)
-        bias_ref[:, span] = total[:1]
+        total = jnp.dot(both, weight, preferred_element_type=F32)
+        bias_ref[:, span] = total[:1] + total[8:9]
 
 
 def fold_weight(scale, shift, own, other):
@@ -120,7 +120,7 @@
             jax.ShapeDtypeStruct((dmodel, 2 * parts * width), BF16),
             jax.ShapeDtypeStruct((1, 2 * parts * width), F32),
         ],
-        compiler_params=pltpu.CompilerParams(vmem_limit_bytes=20 * MIB),
+        compiler_params=pltpu.CompilerParams(vmem_limit_bytes=14 * MIB),
         name="fold_weight",
     )(scale.reshape(dmodel, 1), shift.reshape(1, dmodel), own, other)
 
@@ -129,17 +129,13 @@
     weight_ref, bias_ref, column_ref, spot_ref, other_spot_ref, got_ref = refs[:6]
     token_refs, (pair_ref, send_ref, query_ref) = refs[6 : 6 + count], refs[6 + count :]
     width = query_ref.shape[1]
-    base = 0
-    total = jnp.zeros(query_ref.shape, F32)
-    for token_ref in token_refs:
-        here = slice(base, base + token_ref.shape[0])
-        base += token_ref.shape[0]
-        qkv = jnp.dot(token_ref[...], weight_ref[...], preferred_element_type=F32) + bias_ref[...]
-        qkv = qkv.astype(BF16)
-        pair_ref[here, :] = qkv[:, width : 3 * width]
-        send_ref[here, :] = qkv[:, 3 * width :]
-        pick = onehot(column_ref[...] == spot_ref[:, here])
-        total += jnp.dot(pick, qkv[:, :width], preferred_element_type=F32)
+    tokens = jnp.concatenate([token_ref[...] for token_ref in token_refs], axis=0)
+    qkv = jnp.dot(tokens, weight_ref[...], preferred_element_type=F32) + bias_ref[...]
+    qkv = qkv.astype(BF16)
+    pair_ref[...] = qkv[:, width : 3 * width]
+    send_ref[...] = qkv[:, 3 * width :]
+    pick = onehot(column_ref[...] == spot_ref[...])
+    total = jnp.dot(pick, qkv[:, :width], preferred_element_type=F32)
     pick = onehot(column_ref[...] == other_spot_ref[...])
     total += jnp.dot(pick, got_ref[:, :width], preferred_element_type=F32)
     query_ref[...] = total.astype(BF16)
@@ -149,17 +145,13 @@
     weight_ref, bias_ref, column_ref, spot_ref = refs[:4]
     token_refs, (pair_ref, send_ref, query_ref) = refs[4 : 4 + count], refs[4 + count :]
     width = query_ref.shape[1]
-    base = 0
-    total = jnp.zeros(query_ref.shape, F32)
-    for token_ref in token_refs:
-        here = slice(base, base + token_ref.shape[0])
-        base += token_ref.shape[0]
-        qkv = jnp.dot(token_ref[...], weight_ref[...], preferred_element_type=F32) + bias_ref[...]
-        qkv = qkv.astype(BF16)
-        pair_ref[here, :] = qkv[:, width : 3 * width]
-        send_ref[here, :] = qkv[:, 3 * width :]
-        pick = onehot(column_ref[...] == spot_ref[:, here])
-        total += jnp.dot(pick, qkv[:, :width], preferred_element_type=F32)
+    tokens = jnp.concatenate([token_ref[...] for token_ref in token_refs], axis=0)
+    qkv = jnp.dot(tokens, weight_ref[...], preferred_element_type=F32) + bias_ref[...]
+    qkv = qkv.astype(BF16)
+    pair_ref[...] = qkv[:, width : 3 * width]
+    send_ref[...] = qkv[:, 3 * width :]
+    pick = onehot(column_ref[...] == spot_ref[...])
+    total = jnp.dot(pick, qkv[:, :width], preferred_element_type=F32)
     query_ref[...] = total.astype(BF16)
 
 
@@ -177,7 +169,7 @@
             jax.ShapeDtypeStruct((rows, 3 * width), BF16),
             jax.ShapeDtypeStruct((column.shape[0], width), BF16),
         ],
-        compiler_params=pltpu.CompilerParams(vmem_limit_bytes=20 * MIB),
+        compiler_params=pltpu.CompilerParams(vmem_limit_bytes=14 * MIB),
         cost_estimate=pl.CostEstimate(
             flops=4 * rows * weight.size, bytes_accessed=8 * MIB, transcendentals=0
         ),
@@ -247,7 +239,7 @@
             pltpu.VMEM((slots, width), F32),
             pltpu.VMEM((slots, width), BF16),
         ],
-        compiler_params=pltpu.CompilerParams(vmem_limit_bytes=28 * MIB),
+        compiler_params=pltpu.CompilerParams(vmem_limit_bytes=20 * MIB),
         name="attend",
     )(column, row, spots, targets, *pairs, *received, *queries)
 

time: 106 us -> 106 us (level)
  Pallas kernels: 24.7 us -> 23.6 us
  transfers between devices with their start and end apart: 13 -> 13, of which waited for: 4 -> 4; matrix products, arithmetic and copies ran while one was open for 3% -> 3% of each run, Pallas kernels for 14% -> 13%
where the time goes in v3:
time: 106 us; the launch traced here: 105 us
  starting transfers between devices  58.1 us (55%)
  Pallas kernels  23.6 us (22%)
  waiting for transfers between devices  13.9 us (13%)
  local copies, waits for them, and re-layouts  7.04 us (7%)
  between operations  1.61 us (2%)
    ppermute x1, starting transfers between devices, shards(): up1 = lax.ppermute(normed, 'seq', onward)  11.5 us
    pallas_call x3, Pallas kernels, project(): pl.pallas_call(functools.partial(body, len(tokens)), in_specs=[vmem] * (4...  9.72 us
    all_to_all x1, starting transfers between devices, shards(): got = lax.all_to_all(after(sent, normed), 'fsdp', 0, 0, tiled=True)  9.67 us
    pallas_call x1, Pallas kernels, attend(): pl.pallas_call(functools.partial(attend_kernel, len(pairs)), in_specs=[vm...  8.55 us
    all_to_all x1, waiting for transfers between devices, shards(): lax.all_to_all(after(part, up1), 'fsdp', 0, 0, tiled=True)  8.01 us
    ppermute x1, starting transfers between devices, shards(): got_first = lax.ppermute(first[1], 'seq', swap)  5.07 us
    all_to_all x1, starting transfers between devices, shards(): lax.all_to_all(after(part, up1), 'fsdp', 0, 0, tiled=True)  5.07 us
    ppermute x1, starting transfers between devices, shards(): up4 = lax.ppermute(after(up3, *first), 'seq', onward)  4.85 us
  transfers between devices with their start and end apart: 13, of which 4 were waited for; matrix products, arithmetic and copies ran while one was open for 3% of the time, Pallas kernels for 13%

profile of v3, /device:TPU:1, one launch (start us, length us, event | category | flops | bytes accessed | tf_op | source)
XLA Modules:
  0.0 105.0 jit_solution(1753210453800231258)
XLA Ops:
  0.0 0.0 copy-start
  0.7 1.1 %copy-done.3 = bf16[1,128,2432]{2,1,0:T(8,128)(2,1)S(1)} copy-done((bf16[1,128,2432]{2,1,0:T(8,128)(2,1)S(1)}, bf16[1,128,2432]{2,1,0:T(8,128)(2,1)}, u32[]{:S(2)}) %copy-start.3) | copy-done | bytes 622616
  1.8 1.1 %copy-done.4 = bf16[1,128,2432]{2,1,0:T(8,128)(2,1)S(1)} copy-done((bf16[1,128,2432]{2,1,0:T(8,128)(2,1)S(1)}, bf16[1,128,2432]{2,1,0:T(8,128)(2,1)}, u32[]{:S(2)}) %copy-start.4) | copy-done | bytes 622616
  2.8 0.6 normalize.1.refs_4_
  3.5 11.5 %collective-permute-start = (bf16[128,2432]{1,0:T(8,128)(2,1)S(1)}, bf16[128,2432]{1,0:T(8,128)(2,1)S(1)}, u32[]{:S(2)}, u32[]{:S(2)}) collective-permute-start(bf16[128,2432]{1,0:T(8,128)(2,1)S(1)} %normalize.1.refs_4_), channel_id=1, source_target_pairs={{0,64},{32,480},{64,128},{96,32},{128,192},{160,96},{192,256},{224... | collective-permute-start | bytes 1867784 | tf_op jit(solution)/shard_map/ppermute | solution.py:273
  15.0 1.9 %collective-permute-start.2 = (bf16[128,2432]{1,0:T(8,128)(2,1)S(1)}, bf16[128,2432]{1,0:T(8,128)(2,1)}, u32[]{:S(2)}, u32[]{:S(2)}) collective-permute-start(bf16[128,2432]{1,0:T(8,128)(2,1)S(1)} %normalize.1.refs_4_), channel_id=1, source_target_pairs={{0,448},{32,96},{64,0},{96,160},{128,64},{160,224},{192,128},{224,... | collective-permute-start | bytes 1867784 | tf_op jit(solution)/shard_map/ppermute | solution.py:274
  17.0 1.5 %pack_rows.1 = bf16[32,48,128]{2,1,0:T(8,128)(2,1)} custom-call(s32[1]{0:T(128)S(6)} %copy.30.stamp_ref, s32[1,512]{1,0:T(1,128)S(1)} %bitcast.16, s32[1,512]{1,0:T(1,128)S(1)} %bitcast.17, bf16[512,128]{1,0:T(8,128)(2,1)S(1)} %copy-done.5), custom_call_target="tpu_custom_call" | custom-call | tf_op jit(solution)/shard_map/pack_rows/pallas_call | solution.py:87
  18.4 9.7 %all-to-all-start = ((bf16[32,48,128]{2,1,0:T(8,128)(2,1)}), bf16[32,48,128]{2,1,0:T(8,128)(2,1)S(1)}, u32[]{:S(2)}, u32[]{:S(2)}) async-start(bf16[32,48,128]{2,1,0:T(8,128)(2,1)} %pack_rows.1), calls=%async_computation | async-start | bytes 786432 | tf_op jit(solution)/shard_map/all_to_all | solution.py:278
  28.1 3.1 %collective-permute-start.1 = (bf16[3,2432,128]{2,1,0:T(8,128)(2,1)}, bf16[3,2432,128]{2,1,0:T(8,128)(2,1)}, u32[]{:S(2)}, u32[]{:S(2)}) collective-permute-start(bf16[3,2432,128]{2,1,0:T(8,128)(2,1)} %bitcast.7.own_ref), channel_id=1, source_target_pairs={{0,32},{32,0},{64,96},{96,64},{128,160},{160,128},{192,224},{224,1... | collective-permute-start | bytes 5603336 | tf_op jit(solution)/shard_map/ppermute | solution.py:280
  31.7 0.0 collective-permute-done.refs_5_
  31.7 3.6 %collective-permute-start.3 = (bf16[128,2432]{1,0:T(8,128)(2,1)S(1)}, bf16[128,2432]{1,0:T(8,128)(2,1)}, u32[]{:S(2)}, u32[]{:S(2)}) collective-permute-start(bf16[128,2432]{1,0:T(8,128)(2,1)S(1)} %collective-permute-done.refs_5_), channel_id=1, source_target_pairs={{0,64},{32,480},{64,128},{96,32},{128,192},{160,96},{192,256},{224... | collective-permute-start | bytes 1867784 | tf_op jit(solution)/shard_map/ppermute | solution.py:281
  35.3 0.0 collective-permute-done.2.refs_6_
  35.4 1.9 %collective-permute-start.4 = (bf16[128,2432]{1,0:T(8,128)(2,1)}, bf16[128,2432]{1,0:T(8,128)(2,1)}, u32[]{:S(2)}, u32[]{:S(2)}) collective-permute-start(bf16[128,2432]{1,0:T(8,128)(2,1)} %collective-permute-done.2.refs_6_), channel_id=1, source_target_pairs={{0,448},{32,96},{64,0},{96,160},{128,64},{160,224},{192,128},{224,... | collective-permute-start | bytes 1867784 | tf_op jit(solution)/shard_map/ppermute | solution.py:282
  37.3 4.5 %all-to-all-done = bf16[32,48,128]{2,1,0:T(8,128)(2,1)S(1)} async-done(((bf16[32,48,128]{2,1,0:T(8,128)(2,1)}), bf16[32,48,128]{2,1,0:T(8,128)(2,1)S(1)}, u32[]{:S(2)}, u32[]{:S(2)}) %all-to-all-start) | async-done | bytes 393248 | tf_op jit(solution)/shard_map/all_to_all | solution.py:278
  41.8 0.2 fusion.3
  42.0 0.1 multiply_cosine_fusion
  42.2 0.1 fusion
  42.3 0.7 copy.14
  43.0 5.1 %all-to-all-start.1 = ((f32[32,1,152]{2,1,0:T(1,128)}), f32[32,1,152]{2,1,0:T(1,128)S(1)}, u32[]{:S(2)}, u32[]{:S(2)}) async-start(f32[32,1,152]{2,1,0:T(1,128)} %copy.14), calls=%async_computation.1 | async-start | bytes 65536 | tf_op jit(solution)/shard_map/all_to_all | solution.py:293
  48.1 0.1 fusion.5
  48.1 0.5 reshape.62.refs_2_.column_ref
  48.7 8.0 %all-to-all-done.1 = f32[32,1,152]{2,1,0:T(1,128)S(1)} async-done(((f32[32,1,152]{2,1,0:T(1,128)}), f32[32,1,152]{2,1,0:T(1,128)S(1)}, u32[]{:S(2)}, u32[]{:S(2)}) %all-to-all-start.1) | async-done | bytes 19488 | tf_op jit(solution)/shard_map/all_to_all | solution.py:293
  56.7 0.1 slice_reduce_fusion
  56.8 0.4 reshape.61.scale_ref
  57.2 0.1 reshape.59.shift_ref
  57.3 0.0 collective-permute-done.4.refs_8_
  57.3 1.9 %collective-permute-start.7 = (bf16[128,2432]{1,0:T(8,128)(2,1)}, bf16[128,2432]{1,0:T(8,128)(2,1)}, u32[]{:S(2)}, u32[]{:S(2)}) collective-permute-start(bf16[128,2432]{1,0:T(8,128)(2,1)} %collective-permute-done.4.refs_8_), channel_id=1, source_target_pairs={{0,448},{32,96},{64,0},{96,160},{128,64},{160,224},{192,128},{224,... | collective-permute-start | bytes 1867784 | tf_op jit(solution)/shard_map/ppermute | solution.py:294
  59.2 0.0 collective-permute-done.3.refs_7_
  59.2 4.7 %collective-permute-start.6 = (bf16[128,2432]{1,0:T(8,128)(2,1)}, bf16[128,2432]{1,0:T(8,128)(2,1)}, u32[]{:S(2)}, u32[]{:S(2)}) collective-permute-start(bf16[128,2432]{1,0:T(8,128)(2,1)} %collective-permute-done.3.refs_7_), channel_id=1, source_target_pairs={{0,64},{32,480},{64,128},{96,32},{128,192},{160,96},{192,256},{224... | collective-permute-start | bytes 1867784 | tf_op jit(solution)/shard_map/ppermute | solution.py:292
  63.9 0.0 collective-permute-done.1.other_ref
  63.9 3.2 %fold_weight.1 = (bf16[2432,768]{1,0:T(8,128)(2,1)S(1)}, f32[1,768]{1,0:T(1,128)S(1)}) custom-call(f32[2432,1]{1,0:T(8,128)S(1)} %reshape.61.scale_ref, f32[1,2432]{1,0:T(1,128)S(1)} %reshape.59.shift_ref, bf16[3,2432,128]{2,1,0:T(8,128)(2,1)} %bitcast.7.own_ref, bf16[3,2432,128]{2,1,0:T(8,128)(2,1)} %collective-permute-done.1.other_ref), custom_call_target="tpu_custom_call" | custom-call | tf_op jit(solution)/shard_map/fold_weight/pallas_call | solution.py:115
  67.2 5.9 %project.3 = (bf16[640,256]{1,0:T(8,128)(2,1)S(1)}, bf16[640,384]{1,0:T(8,128)(2,1)S(1)}, bf16[1024,128]{1,0:T(8,128)(2,1)S(1)}) custom-call(bf16[2432,768]{1,0:T(8,128)(2,1)S(1)} %get-tuple-element.24.refs_0_, f32[1,768]{1,0:T(1,128)S(1)} %get-tuple-element.25.refs_1_, s32[1024,1]{1,0:T(8,128)S(1)} %reshape.62.refs_2_.column_ref, ...), custom_call_target="tpu_custom_call" | custom-call | flops 4781506560 | bytes 8388608 | tf_op jit(solution)/shard_map/project/pallas_call | solution.py:163
  73.1 5.1 %collective-permute-start.5 = (bf16[640,384]{1,0:T(8,128)(2,1)S(1)}, bf16[640,384]{1,0:T(8,128)(2,1)S(1)}, u32[]{:S(2)}, u32[]{:S(2)}) collective-permute-start(bf16[640,384]{1,0:T(8,128)(2,1)S(1)} %get-tuple-element.27), channel_id=1, source_target_pairs={{0,32},{32,0},{64,96},{96,64},{128,160},{160,128},{192,224},{224,1... | collective-permute-start | bytes 1474568 | tf_op jit(solution)/shard_map/ppermute | solution.py:301
  78.4 0.0 collective-permute-done.6.refs_6_
  78.4 4.9 %collective-permute-start.9 = (bf16[128,2432]{1,0:T(8,128)(2,1)}, bf16[128,2432]{1,0:T(8,128)(2,1)S(1)}, u32[]{:S(2)}, u32[]{:S(2)}) collective-permute-start(bf16[128,2432]{1,0:T(8,128)(2,1)} %collective-permute-done.6.refs_6_), channel_id=1, source_target_pairs={{0,64},{32,480},{64,128},{96,32},{128,192},{160,96},{192,256},{224... | collective-permute-start | bytes 1867784 | tf_op jit(solution)/shard_map/ppermute | solution.py:302
  83.3 0.0 collective-permute-done.7.refs_7_
  83.3 0.0 collective-permute-done.5.refs_5_.refs_3_
  83.3 2.0 %copy-done.2 = bf16[2432,768]{1,0:T(8,128)(2,1)S(1)} copy-done((bf16[2432,768]{1,0:T(8,128)(2,1)S(1)}, bf16[2432,768]{1,0:T(8,128)(2,1)}, u32[]{:S(2)}) %copy-start.2) | copy-done | bytes 3735576
  85.4 2.9 %project.4 = (bf16[256,256]{1,0:T(8,128)(2,1)S(1)}, bf16[256,384]{1,0:T(8,128)(2,1)S(1)}, bf16[1024,128]{1,0:T(8,128)(2,1)S(1)}) custom-call(bf16[2432,768]{1,0:T(8,128)(2,1)S(1)} %copy-done.2, f32[1,768]{1,0:T(1,128)S(1)} %get-tuple-element.25.refs_1_, s32[1024,1]{1,0:T(8,128)S(1)} %reshape.62.refs_2_.column_ref, s32[1,256]{1,0:T(1,128)S(1)} %bitcast.18, ...), custom_call_target="tpu_custom_call" | custom-call | flops 1912602624 | bytes 8388608 | tf_op jit(solution)/shard_map/project/pallas_call | solution.py:163
  88.3 1.9 %collective-permute-start.8 = (bf16[256,384]{1,0:T(8,128)(2,1)S(1)}, bf16[256,384]{1,0:T(8,128)(2,1)S(1)}, u32[]{:S(2)}, u32[]{:S(2)}) collective-permute-start(bf16[256,384]{1,0:T(8,128)(2,1)S(1)} %get-tuple-element.30), channel_id=1, source_target_pairs={{0,32},{32,0},{64,96},{96,64},{128,160},{160,128},{192,224},{224,1... | collective-permute-start | bytes 589832 | tf_op jit(solution)/shard_map/ppermute | solution.py:306
  90.3 0.5 collective-permute-done.9.refs_6_
  90.7 0.9 collective-permute-done.8.refs_5_.refs_4_
  91.6 0.9 project.5
  92.6 2.8 %collective-permute-start.10 = (bf16[128,384]{1,0:T(8,128)(2,1)S(1)}, bf16[128,384]{1,0:T(8,128)(2,1)S(1)}, u32[]{:S(2)}, u32[]{:S(2)}) collective-permute-start(bf16[128,384]{1,0:T(8,128)(2,1)S(1)} %get-tuple-element.34), channel_id=1, source_target_pairs={{0,32},{32,0},{64,96},{96,64},{128,160},{160,128},{192,224},{224,1... | collective-permute-start | bytes 294920 | tf_op jit(solution)/shard_map/ppermute | solution.py:308
  95.4 0.1 reshape.56.row_ref
  95.5 1.0 slice.39
  96.4 0.0 collective-permute-done.10.refs_5_
  96.4 8.6 %attend.1 = bf16[2048,128]{1,0:T(8,128)(2,1)} custom-call(s32[1024,1]{1,0:T(8,128)S(1)} %reshape.62.refs_2_.column_ref, s32[1,1024]{1,0:T(1,128)S(1)} %reshape.56.row_ref, s32[1,128]{1,0:T(1,128)S(1)} %iota_add_fusion.5.spot_ref, bf16[1024,128]{1,0:T(8,128)(2,1)S(1)} %bitcast.12, bf16[640,256]{1,0:T(8,128)(2,1)S(1)} %get-tuple-element.26.refs_0_, ...), custom_call_target="tpu_custom_call" | custom-call | tf_op jit(solution)/shard_map/attend/pallas_call | solution.py:230
  (40 shorter events, 0.2 us)
Async XLA Ops:
  0.0 42.2 %copy-start = (bf16[256,152]{0,1:T(8,128)(2,1)S(1)}, bf16[256,152]{0,1:T(8,128)(2,1)}, u32[]{:S(2)}) copy-start(bf16[256,152]{0,1:T(8,128)(2,1)} %param.11) | copy-start | bytes 233476
  0.0 16.9 %copy-start.6 = (s32[512,1]{0,1:T(1,128)S(1)}, s32[512,1]{0,1:T(1,128)}, u32[]{:S(2)}) copy-start(s32[512,1]{0,1:T(1,128)} %param.14) | copy-start | bytes 6148
  0.0 16.9 %copy-start.7 = (s32[512]{0:T(512)S(1)}, s32[512]{0:T(512)}, u32[]{:S(2)}) copy-start(s32[512]{0:T(512)} %param.15) | copy-start | bytes 6148
  0.7 1.1 %copy-start.3 = (bf16[1,128,2432]{2,1,0:T(8,128)(2,1)S(1)}, bf16[1,128,2432]{2,1,0:T(8,128)(2,1)}, u32[]{:S(2)}) copy-start(bf16[1,128,2432]{2,1,0:T(8,128)(2,1)} %param.8) | copy-start | bytes 1867780
  1.8 1.1 %copy-start.4 = (bf16[1,128,2432]{2,1,0:T(8,128)(2,1)S(1)}, bf16[1,128,2432]{2,1,0:T(8,128)(2,1)}, u32[]{:S(2)}) copy-start(bf16[1,128,2432]{2,1,0:T(8,128)(2,1)} %param.9) | copy-start | bytes 1867780
  2.8 14.1 %copy-start.5 = (bf16[512,128]{1,0:T(8,128)(2,1)S(1)}, bf16[512,128]{1,0:T(8,128)(2,1)}, u32[]{:S(2)}) copy-start(bf16[512,128]{1,0:T(8,128)(2,1)} %target_ref.1) | copy-start | bytes 393220
  3.5 28.2 %collective-permute-start = (bf16[128,2432]{1,0:T(8,128)(2,1)S(1)}, bf16[128,2432]{1,0:T(8,128)(2,1)S(1)}, u32[]{:S(2)}, u32[]{:S(2)}) collective-permute-start(bf16[128,2432]{1,0:T(8,128)(2,1)S(1)} %normalize.1.refs_4_), channel_id=1, source_target_pairs={{0,64},{32,480},{64,128},{96,32},{128,192},{160,96},{192,256},{224... | collective-permute-start | bytes 1867784 | tf_op jit(solution)/shard_map/ppermute | solution.py:273
  15.0 20.3 %collective-permute-start.2 = (bf16[128,2432]{1,0:T(8,128)(2,1)S(1)}, bf16[128,2432]{1,0:T(8,128)(2,1)}, u32[]{:S(2)}, u32[]{:S(2)}) collective-permute-start(bf16[128,2432]{1,0:T(8,128)(2,1)S(1)} %normalize.1.refs_4_), channel_id=1, source_target_pairs={{0,448},{32,96},{64,0},{96,160},{128,64},{160,224},{192,128},{224,... | collective-permute-start | bytes 1867784 | tf_op jit(solution)/shard_map/ppermute | solution.py:274
  18.4 23.4 %all-to-all-start = ((bf16[32,48,128]{2,1,0:T(8,128)(2,1)}), bf16[32,48,128]{2,1,0:T(8,128)(2,1)S(1)}, u32[]{:S(2)}, u32[]{:S(2)}) async-start(bf16[32,48,128]{2,1,0:T(8,128)(2,1)} %pack_rows.1), calls=%async_computation | async-start | bytes 786432 | tf_op jit(solution)/shard_map/all_to_all | solution.py:278
  28.1 35.8 %collective-permute-start.1 = (bf16[3,2432,128]{2,1,0:T(8,128)(2,1)}, bf16[3,2432,128]{2,1,0:T(8,128)(2,1)}, u32[]{:S(2)}, u32[]{:S(2)}) collective-permute-start(bf16[3,2432,128]{2,1,0:T(8,128)(2,1)} %bitcast.7.own_ref), channel_id=1, source_target_pairs={{0,32},{32,0},{64,96},{96,64},{128,160},{160,128},{192,224},{224,1... | collective-permute-start | bytes 5603336 | tf_op jit(solution)/shard_map/ppermute | solution.py:280
  31.7 32.2 %copy-start.8 = (bf16[128,2432]{1,0:T(8,128)(2,1)}, bf16[128,2432]{1,0:T(8,128)(2,1)S(1)}, u32[]{:S(2)}) copy-start(bf16[128,2432]{1,0:T(8,128)(2,1)S(1)} %collective-permute-done.refs_5_) | copy-start | bytes 1867780
  31.7 27.5 %collective-permute-start.3 = (bf16[128,2432]{1,0:T(8,128)(2,1)S(1)}, bf16[128,2432]{1,0:T(8,128)(2,1)}, u32[]{:S(2)}, u32[]{:S(2)}) collective-permute-start(bf16[128,2432]{1,0:T(8,128)(2,1)S(1)} %collective-permute-done.refs_5_), channel_id=1, source_target_pairs={{0,64},{32,480},{64,128},{96,32},{128,192},{160,96},{192,256},{224... | collective-permute-start | bytes 1867784 | tf_op jit(solution)/shard_map/ppermute | solution.py:281
  35.4 21.9 %collective-permute-start.4 = (bf16[128,2432]{1,0:T(8,128)(2,1)}, bf16[128,2432]{1,0:T(8,128)(2,1)}, u32[]{:S(2)}, u32[]{:S(2)}) collective-permute-start(bf16[128,2432]{1,0:T(8,128)(2,1)} %collective-permute-done.2.refs_6_), channel_id=1, source_target_pairs={{0,448},{32,96},{64,0},{96,160},{128,64},{160,224},{192,128},{224,... | collective-permute-start | bytes 1867784 | tf_op jit(solution)/shard_map/ppermute | solution.py:282
  41.8 15.0 %copy-start.10 = (bf16[32,48,128]{2,1,0:T(8,128)(2,1)}, bf16[32,48,128]{2,1,0:T(8,128)(2,1)S(1)}, u32[]{:S(2)}) copy-start(bf16[32,48,128]{2,1,0:T(8,128)(2,1)S(1)} %all-to-all-done) | copy-start | bytes 1179652
  43.0 13.7 %all-to-all-start.1 = ((f32[32,1,152]{2,1,0:T(1,128)}), f32[32,1,152]{2,1,0:T(1,128)S(1)}, u32[]{:S(2)}, u32[]{:S(2)}) async-start(f32[32,1,152]{2,1,0:T(1,128)} %copy.14), calls=%async_computation.1 | async-start | bytes 65536 | tf_op jit(solution)/shard_map/all_to_all | solution.py:293
  57.3 26.0 %collective-permute-start.7 = (bf16[128,2432]{1,0:T(8,128)(2,1)}, bf16[128,2432]{1,0:T(8,128)(2,1)}, u32[]{:S(2)}, u32[]{:S(2)}) collective-permute-start(bf16[128,2432]{1,0:T(8,128)(2,1)} %collective-permute-done.4.refs_8_), channel_id=1, source_target_pairs={{0,448},{32,96},{64,0},{96,160},{128,64},{160,224},{192,128},{224,... | collective-permute-start | bytes 1867784 | tf_op jit(solution)/shard_map/ppermute | solution.py:294
  59.2 19.1 %collective-permute-start.6 = (bf16[128,2432]{1,0:T(8,128)(2,1)}, bf16[128,2432]{1,0:T(8,128)(2,1)}, u32[]{:S(2)}, u32[]{:S(2)}) collective-permute-start(bf16[128,2432]{1,0:T(8,128)(2,1)} %collective-permute-done.3.refs_7_), channel_id=1, source_target_pairs={{0,64},{32,480},{64,128},{96,32},{128,192},{160,96},{192,256},{224... | collective-permute-start | bytes 1867784 | tf_op jit(solution)/shard_map/ppermute | solution.py:292
  63.9 3.2 %copy-start.9 = (bf16[128,2432]{1,0:T(8,128)(2,1)S(1)}, bf16[128,2432]{1,0:T(8,128)(2,1)}, u32[]{:S(2)}) copy-start(bf16[128,2432]{1,0:T(8,128)(2,1)} %copy-done.8) | copy-start | bytes 1867780
  67.2 5.9 %copy-start.1 = (bf16[2432,768]{1,0:T(8,128)(2,1)}, bf16[2432,768]{1,0:T(8,128)(2,1)S(1)}, u32[]{:S(2)}) copy-start(bf16[2432,768]{1,0:T(8,128)(2,1)S(1)} %get-tuple-element.24.refs_0_) | copy-start | bytes 11206660
  73.1 10.2 %collective-permute-start.5 = (bf16[640,384]{1,0:T(8,128)(2,1)S(1)}, bf16[640,384]{1,0:T(8,128)(2,1)S(1)}, u32[]{:S(2)}, u32[]{:S(2)}) collective-permute-start(bf16[640,384]{1,0:T(8,128)(2,1)S(1)} %get-tuple-element.27), channel_id=1, source_target_pairs={{0,32},{32,0},{64,96},{96,64},{128,160},{160,128},{192,224},{224,1... | collective-permute-start | bytes 1474568 | tf_op jit(solution)/shard_map/ppermute | solution.py:301
  78.4 12.3 %collective-permute-start.9 = (bf16[128,2432]{1,0:T(8,128)(2,1)}, bf16[128,2432]{1,0:T(8,128)(2,1)S(1)}, u32[]{:S(2)}, u32[]{:S(2)}) collective-permute-start(bf16[128,2432]{1,0:T(8,128)(2,1)} %collective-permute-done.6.refs_6_), channel_id=1, source_target_pairs={{0,64},{32,480},{64,128},{96,32},{128,192},{160,96},{192,256},{224... | collective-permute-start | bytes 1867784 | tf_op jit(solution)/shard_map/ppermute | solution.py:302
  83.3 2.1 %copy-start.2 = (bf16[2432,768]{1,0:T(8,128)(2,1)S(1)}, bf16[2432,768]{1,0:T(8,128)(2,1)}, u32[]{:S(2)}) copy-start(bf16[2432,768]{1,0:T(8,128)(2,1)} %copy-done.1) | copy-start | bytes 11206660
  88.3 3.3 %collective-permute-start.8 = (bf16[256,384]{1,0:T(8,128)(2,1)S(1)}, bf16[256,384]{1,0:T(8,128)(2,1)S(1)}, u32[]{:S(2)}, u32[]{:S(2)}) collective-permute-start(bf16[256,384]{1,0:T(8,128)(2,1)S(1)} %get-tuple-element.30), channel_id=1, source_target_pairs={{0,32},{32,0},{64,96},{96,64},{128,160},{160,128},{192,224},{224,1... | collective-permute-start | bytes 589832 | tf_op jit(solution)/shard_map/ppermute | solution.py:306
  92.6 3.9 %collective-permute-start.10 = (bf16[128,384]{1,0:T(8,128)(2,1)S(1)}, bf16[128,384]{1,0:T(8,128)(2,1)S(1)}, u32[]{:S(2)}, u32[]{:S(2)}) collective-permute-start(bf16[128,384]{1,0:T(8,128)(2,1)S(1)} %get-tuple-element.34), channel_id=1, source_target_pairs={{0,32},{32,0},{64,96},{96,64},{128,160},{160,128},{192,224},{224,1... | collective-permute-start | bytes 294920 | tf_op jit(solution)/shard_map/ppermute | solution.py:308

commit v4 on v3

--- a/solution.py
+++ b/solution.py
@@ -198,7 +198,7 @@
     query += jnp.dot(pick, got_refs[-1][:, :width], preferred_element_type=F32)
     query_ref[...] = query
     factor = math.log2(math.e) / math.sqrt(HEAD_DIM)
-    part = 256
+    part = 512
     half = lax.broadcasted_iota(jnp.int32, (part, width), 1) < HEAD_DIM
     for start in range(0, slots, part):
         query = query_ref[start : start + part, :]
@@ -215,6 +215,7 @@
         attended = jnp.where(half, outs[0], outs[1])
         target = target_ref[start : start + part, :].astype(F32)
         diff_ref[start : start + part, :] = (attended - target).astype(BF16)
+    part = 256
     for start in range(0, length, part):
         spots = lax.broadcasted_iota(jnp.int32, (part, slots), 0) + start
         spread = onehot(row_ref[...] == spots)
@@ -239,7 +240,7 @@
             pltpu.VMEM((slots, width), F32),
             pltpu.VMEM((slots, width), BF16),
         ],
-        compiler_params=pltpu.CompilerParams(vmem_limit_bytes=20 * MIB),
+        compiler_params=pltpu.CompilerParams(vmem_limit_bytes=28 * MIB),
         name="attend",
     )(column, row, spots, targets, *pairs, *received, *queries)
 

time: 106 us -> 106 us (level)
  no operation moved by 1% of the time
where the time goes in v4:
time: 106 us; the launch traced here: 105 us
  starting transfers between devices  58.1 us (55%)
  Pallas kernels  23.5 us (22%)
  waiting for transfers between devices  13.9 us (13%)
  local copies, waits for them, and re-layouts  7.04 us (7%)
  between operations  1.61 us (2%)
    ppermute x1, starting transfers between devices, shards(): up1 = lax.ppermute(normed, 'seq', onward)  11.5 us
    pallas_call x3, Pallas kernels, project(): pl.pallas_call(functools.partial(body, len(tokens)), in_specs=[vmem] * (4...  9.72 us
    all_to_all x1, starting transfers between devices, shards(): got = lax.all_to_all(after(sent, normed), 'fsdp', 0, 0, tiled=True)  9.67 us
    pallas_call x1, Pallas kernels, attend(): pl.pallas_call(functools.partial(attend_kernel, len(pairs)), in_specs=[vm...  8.44 us
    all_to_all x1, waiting for transfers between devices, shards(): lax.all_to_all(after(part, up1), 'fsdp', 0, 0, tiled=True)  8.01 us
    ppermute x1, starting transfers between devices, shards(): got_first = lax.ppermute(first[1], 'seq', swap)  5.07 us
    all_to_all x1, starting transfers between devices, shards(): lax.all_to_all(after(part, up1), 'fsdp', 0, 0, tiled=True)  5.07 us
    ppermute x1, starting transfers between devices, shards(): up4 = lax.ppermute(after(up3, *first), 'seq', onward)  4.85 us
  transfers between devices with their start and end apart: 13, of which 4 were waited for; matrix products, arithmetic and copies ran while one was open for 3% of the time, Pallas kernels for 13%

profile of v4, /device:TPU:1, one launch (start us, length us, event | category | flops | bytes accessed | tf_op | source)
XLA Modules:
  0.0 104.9 jit_solution(17963666575877379249)
XLA Ops:
  0.0 0.0 copy-start
  0.7 1.1 %copy-done.3 = bf16[1,128,2432]{2,1,0:T(8,128)(2,1)S(1)} copy-done((bf16[1,128,2432]{2,1,0:T(8,128)(2,1)S(1)}, bf16[1,128,2432]{2,1,0:T(8,128)(2,1)}, u32[]{:S(2)}) %copy-start.3) | copy-done | bytes 622616
  1.8 1.1 %copy-done.4 = bf16[1,128,2432]{2,1,0:T(8,128)(2,1)S(1)} copy-done((bf16[1,128,2432]{2,1,0:T(8,128)(2,1)S(1)}, bf16[1,128,2432]{2,1,0:T(8,128)(2,1)}, u32[]{:S(2)}) %copy-start.4) | copy-done | bytes 622616
  2.8 0.6 normalize.1.refs_4_
  3.5 11.5 %collective-permute-start = (bf16[128,2432]{1,0:T(8,128)(2,1)S(1)}, bf16[128,2432]{1,0:T(8,128)(2,1)S(1)}, u32[]{:S(2)}, u32[]{:S(2)}) collective-permute-start(bf16[128,2432]{1,0:T(8,128)(2,1)S(1)} %normalize.1.refs_4_), channel_id=1, source_target_pairs={{0,64},{32,480},{64,128},{96,32},{128,192},{160,96},{192,256},{224... | collective-permute-start | bytes 1867784 | tf_op jit(solution)/shard_map/ppermute | solution.py:274
  15.0 1.9 %collective-permute-start.2 = (bf16[128,2432]{1,0:T(8,128)(2,1)S(1)}, bf16[128,2432]{1,0:T(8,128)(2,1)}, u32[]{:S(2)}, u32[]{:S(2)}) collective-permute-start(bf16[128,2432]{1,0:T(8,128)(2,1)S(1)} %normalize.1.refs_4_), channel_id=1, source_target_pairs={{0,448},{32,96},{64,0},{96,160},{128,64},{160,224},{192,128},{224,... | collective-permute-start | bytes 1867784 | tf_op jit(solution)/shard_map/ppermute | solution.py:275
  17.0 1.5 %pack_rows.1 = bf16[32,48,128]{2,1,0:T(8,128)(2,1)} custom-call(s32[1]{0:T(128)S(6)} %copy.30.stamp_ref, s32[1,512]{1,0:T(1,128)S(1)} %bitcast.16, s32[1,512]{1,0:T(1,128)S(1)} %bitcast.17, bf16[512,128]{1,0:T(8,128)(2,1)S(1)} %copy-done.5), custom_call_target="tpu_custom_call" | custom-call | tf_op jit(solution)/shard_map/pack_rows/pallas_call | solution.py:87
  18.4 9.7 %all-to-all-start = ((bf16[32,48,128]{2,1,0:T(8,128)(2,1)}), bf16[32,48,128]{2,1,0:T(8,128)(2,1)S(1)}, u32[]{:S(2)}, u32[]{:S(2)}) async-start(bf16[32,48,128]{2,1,0:T(8,128)(2,1)} %pack_rows.1), calls=%async_computation | async-start | bytes 786432 | tf_op jit(solution)/shard_map/all_to_all | solution.py:279
  28.1 3.1 %collective-permute-start.1 = (bf16[3,2432,128]{2,1,0:T(8,128)(2,1)}, bf16[3,2432,128]{2,1,0:T(8,128)(2,1)}, u32[]{:S(2)}, u32[]{:S(2)}) collective-permute-start(bf16[3,2432,128]{2,1,0:T(8,128)(2,1)} %bitcast.7.own_ref), channel_id=1, source_target_pairs={{0,32},{32,0},{64,96},{96,64},{128,160},{160,128},{192,224},{224,1... | collective-permute-start | bytes 5603336 | tf_op jit(solution)/shard_map/ppermute | solution.py:281
  31.7 0.0 collective-permute-done.refs_5_
  31.7 3.6 %collective-permute-start.3 = (bf16[128,2432]{1,0:T(8,128)(2,1)S(1)}, bf16[128,2432]{1,0:T(8,128)(2,1)}, u32[]{:S(2)}, u32[]{:S(2)}) collective-permute-start(bf16[128,2432]{1,0:T(8,128)(2,1)S(1)} %collective-permute-done.refs_5_), channel_id=1, source_target_pairs={{0,64},{32,480},{64,128},{96,32},{128,192},{160,96},{192,256},{224... | collective-permute-start | bytes 1867784 | tf_op jit(solution)/shard_map/ppermute | solution.py:282
  35.3 0.0 collective-permute-done.2.refs_6_
  35.4 1.9 %collective-permute-start.4 = (bf16[128,2432]{1,0:T(8,128)(2,1)}, bf16[128,2432]{1,0:T(8,128)(2,1)}, u32[]{:S(2)}, u32[]{:S(2)}) collective-permute-start(bf16[128,2432]{1,0:T(8,128)(2,1)} %collective-permute-done.2.refs_6_), channel_id=1, source_target_pairs={{0,448},{32,96},{64,0},{96,160},{128,64},{160,224},{192,128},{224,... | collective-permute-start | bytes 1867784 | tf_op jit(solution)/shard_map/ppermute | solution.py:283
  37.3 4.5 %all-to-all-done = bf16[32,48,128]{2,1,0:T(8,128)(2,1)S(1)} async-done(((bf16[32,48,128]{2,1,0:T(8,128)(2,1)}), bf16[32,48,128]{2,1,0:T(8,128)(2,1)S(1)}, u32[]{:S(2)}, u32[]{:S(2)}) %all-to-all-start) | async-done | bytes 393248 | tf_op jit(solution)/shard_map/all_to_all | solution.py:279
  41.8 0.2 fusion.3
  42.0 0.1 multiply_cosine_fusion
  42.2 0.1 fusion
  42.3 0.7 copy.14
  43.0 5.1 %all-to-all-start.1 = ((f32[32,1,152]{2,1,0:T(1,128)}), f32[32,1,152]{2,1,0:T(1,128)S(1)}, u32[]{:S(2)}, u32[]{:S(2)}) async-start(f32[32,1,152]{2,1,0:T(1,128)} %copy.14), calls=%async_computation.1 | async-start | bytes 65536 | tf_op jit(solution)/shard_map/all_to_all | solution.py:294
  48.1 0.1 fusion.5
  48.1 0.5 reshape.62.refs_2_.column_ref
  48.7 8.0 %all-to-all-done.1 = f32[32,1,152]{2,1,0:T(1,128)S(1)} async-done(((f32[32,1,152]{2,1,0:T(1,128)}), f32[32,1,152]{2,1,0:T(1,128)S(1)}, u32[]{:S(2)}, u32[]{:S(2)}) %all-to-all-start.1) | async-done | bytes 19488 | tf_op jit(solution)/shard_map/all_to_all | solution.py:294
  56.7 0.1 slice_reduce_fusion
  56.8 0.4 reshape.61.scale_ref
  57.2 0.1 reshape.59.shift_ref
  57.3 0.0 collective-permute-done.4.refs_8_
  57.3 1.9 %collective-permute-start.7 = (bf16[128,2432]{1,0:T(8,128)(2,1)}, bf16[128,2432]{1,0:T(8,128)(2,1)}, u32[]{:S(2)}, u32[]{:S(2)}) collective-permute-start(bf16[128,2432]{1,0:T(8,128)(2,1)} %collective-permute-done.4.refs_8_), channel_id=1, source_target_pairs={{0,448},{32,96},{64,0},{96,160},{128,64},{160,224},{192,128},{224,... | collective-permute-start | bytes 1867784 | tf_op jit(solution)/shard_map/ppermute | solution.py:295
  59.2 0.0 collective-permute-done.3.refs_7_
  59.2 4.7 %collective-permute-start.6 = (bf16[128,2432]{1,0:T(8,128)(2,1)}, bf16[128,2432]{1,0:T(8,128)(2,1)}, u32[]{:S(2)}, u32[]{:S(2)}) collective-permute-start(bf16[128,2432]{1,0:T(8,128)(2,1)} %collective-permute-done.3.refs_7_), channel_id=1, source_target_pairs={{0,64},{32,480},{64,128},{96,32},{128,192},{160,96},{192,256},{224... | collective-permute-start | bytes 1867784 | tf_op jit(solution)/shard_map/ppermute | solution.py:293
  63.9 0.0 collective-permute-done.1.other_ref
  63.9 3.2 %fold_weight.1 = (bf16[2432,768]{1,0:T(8,128)(2,1)S(1)}, f32[1,768]{1,0:T(1,128)S(1)}) custom-call(f32[2432,1]{1,0:T(8,128)S(1)} %reshape.61.scale_ref, f32[1,2432]{1,0:T(1,128)S(1)} %reshape.59.shift_ref, bf16[3,2432,128]{2,1,0:T(8,128)(2,1)} %bitcast.7.own_ref, bf16[3,2432,128]{2,1,0:T(8,128)(2,1)} %collective-permute-done.1.other_ref), custom_call_target="tpu_custom_call" | custom-call | tf_op jit(solution)/shard_map/fold_weight/pallas_call | solution.py:115
  67.2 5.9 %project.3 = (bf16[640,256]{1,0:T(8,128)(2,1)S(1)}, bf16[640,384]{1,0:T(8,128)(2,1)S(1)}, bf16[1024,128]{1,0:T(8,128)(2,1)S(1)}) custom-call(bf16[2432,768]{1,0:T(8,128)(2,1)S(1)} %get-tuple-element.24.refs_0_, f32[1,768]{1,0:T(1,128)S(1)} %get-tuple-element.25.refs_1_, s32[1024,1]{1,0:T(8,128)S(1)} %reshape.62.refs_2_.column_ref, ...), custom_call_target="tpu_custom_call" | custom-call | flops 4781506560 | bytes 8388608 | tf_op jit(solution)/shard_map/project/pallas_call | solution.py:163
  73.1 5.1 %collective-permute-start.5 = (bf16[640,384]{1,0:T(8,128)(2,1)S(1)}, bf16[640,384]{1,0:T(8,128)(2,1)S(1)}, u32[]{:S(2)}, u32[]{:S(2)}) collective-permute-start(bf16[640,384]{1,0:T(8,128)(2,1)S(1)} %get-tuple-element.27), channel_id=1, source_target_pairs={{0,32},{32,0},{64,96},{96,64},{128,160},{160,128},{192,224},{224,1... | collective-permute-start | bytes 1474568 | tf_op jit(solution)/shard_map/ppermute | solution.py:302
  78.4 0.0 collective-permute-done.6.refs_6_
  78.4 4.9 %collective-permute-start.9 = (bf16[128,2432]{1,0:T(8,128)(2,1)}, bf16[128,2432]{1,0:T(8,128)(2,1)S(1)}, u32[]{:S(2)}, u32[]{:S(2)}) collective-permute-start(bf16[128,2432]{1,0:T(8,128)(2,1)} %collective-permute-done.6.refs_6_), channel_id=1, source_target_pairs={{0,64},{32,480},{64,128},{96,32},{128,192},{160,96},{192,256},{224... | collective-permute-start | bytes 1867784 | tf_op jit(solution)/shard_map/ppermute | solution.py:303
  83.3 0.0 collective-permute-done.7.refs_7_
  83.3 0.0 collective-permute-done.5.refs_5_.refs_3_
  83.3 2.0 %copy-done.2 = bf16[2432,768]{1,0:T(8,128)(2,1)S(1)} copy-done((bf16[2432,768]{1,0:T(8,128)(2,1)S(1)}, bf16[2432,768]{1,0:T(8,128)(2,1)}, u32[]{:S(2)}) %copy-start.2) | copy-done | bytes 3735576
  85.4 2.9 %project.4 = (bf16[256,256]{1,0:T(8,128)(2,1)S(1)}, bf16[256,384]{1,0:T(8,128)(2,1)S(1)}, bf16[1024,128]{1,0:T(8,128)(2,1)S(1)}) custom-call(bf16[2432,768]{1,0:T(8,128)(2,1)S(1)} %copy-done.2, f32[1,768]{1,0:T(1,128)S(1)} %get-tuple-element.25.refs_1_, s32[1024,1]{1,0:T(8,128)S(1)} %reshape.62.refs_2_.column_ref, s32[1,256]{1,0:T(1,128)S(1)} %bitcast.18, ...), custom_call_target="tpu_custom_call" | custom-call | flops 1912602624 | bytes 8388608 | tf_op jit(solution)/shard_map/project/pallas_call | solution.py:163
  88.3 1.9 %collective-permute-start.8 = (bf16[256,384]{1,0:T(8,128)(2,1)S(1)}, bf16[256,384]{1,0:T(8,128)(2,1)S(1)}, u32[]{:S(2)}, u32[]{:S(2)}) collective-permute-start(bf16[256,384]{1,0:T(8,128)(2,1)S(1)} %get-tuple-element.30), channel_id=1, source_target_pairs={{0,32},{32,0},{64,96},{96,64},{128,160},{160,128},{192,224},{224,1... | collective-permute-start | bytes 589832 | tf_op jit(solution)/shard_map/ppermute | solution.py:307
  90.3 0.5 collective-permute-done.9.refs_6_
  90.7 0.9 collective-permute-done.8.refs_5_.refs_4_
  91.6 0.9 project.5
  92.6 2.8 %collective-permute-start.10 = (bf16[128,384]{1,0:T(8,128)(2,1)S(1)}, bf16[128,384]{1,0:T(8,128)(2,1)S(1)}, u32[]{:S(2)}, u32[]{:S(2)}) collective-permute-start(bf16[128,384]{1,0:T(8,128)(2,1)S(1)} %get-tuple-element.34), channel_id=1, source_target_pairs={{0,32},{32,0},{64,96},{96,64},{128,160},{160,128},{192,224},{224,1... | collective-permute-start | bytes 294920 | tf_op jit(solution)/shard_map/ppermute | solution.py:309
  95.4 0.1 reshape.56.row_ref
  95.5 1.0 slice.39
  96.4 0.0 collective-permute-done.10.refs_5_
  96.4 8.4 %attend.1 = bf16[2048,128]{1,0:T(8,128)(2,1)} custom-call(s32[1024,1]{1,0:T(8,128)S(1)} %reshape.62.refs_2_.column_ref, s32[1,1024]{1,0:T(1,128)S(1)} %reshape.56.row_ref, s32[1,128]{1,0:T(1,128)S(1)} %iota_add_fusion.5.spot_ref, bf16[1024,128]{1,0:T(8,128)(2,1)S(1)} %bitcast.12, bf16[640,256]{1,0:T(8,128)(2,1)S(1)} %get-tuple-element.26.refs_0_, ...), custom_call_target="tpu_custom_call" | custom-call | tf_op jit(solution)/shard_map/attend/pallas_call | solution.py:231
  (40 shorter events, 0.2 us)
Async XLA Ops:
  0.0 42.2 %copy-start = (bf16[256,152]{0,1:T(8,128)(2,1)S(1)}, bf16[256,152]{0,1:T(8,128)(2,1)}, u32[]{:S(2)}) copy-start(bf16[256,152]{0,1:T(8,128)(2,1)} %param.11) | copy-start | bytes 233476
  0.0 16.9 %copy-start.6 = (s32[512,1]{0,1:T(1,128)S(1)}, s32[512,1]{0,1:T(1,128)}, u32[]{:S(2)}) copy-start(s32[512,1]{0,1:T(1,128)} %param.14) | copy-start | bytes 6148
  0.0 16.9 %copy-start.7 = (s32[512]{0:T(512)S(1)}, s32[512]{0:T(512)}, u32[]{:S(2)}) copy-start(s32[512]{0:T(512)} %param.15) | copy-start | bytes 6148
  0.7 1.1 %copy-start.3 = (bf16[1,128,2432]{2,1,0:T(8,128)(2,1)S(1)}, bf16[1,128,2432]{2,1,0:T(8,128)(2,1)}, u32[]{:S(2)}) copy-start(bf16[1,128,2432]{2,1,0:T(8,128)(2,1)} %param.8) | copy-start | bytes 1867780
  1.8 1.1 %copy-start.4 = (bf16[1,128,2432]{2,1,0:T(8,128)(2,1)S(1)}, bf16[1,128,2432]{2,1,0:T(8,128)(2,1)}, u32[]{:S(2)}) copy-start(bf16[1,128,2432]{2,1,0:T(8,128)(2,1)} %param.9) | copy-start | bytes 1867780
  2.8 14.1 %copy-start.5 = (bf16[512,128]{1,0:T(8,128)(2,1)S(1)}, bf16[512,128]{1,0:T(8,128)(2,1)}, u32[]{:S(2)}) copy-start(bf16[512,128]{1,0:T(8,128)(2,1)} %target_ref.1) | copy-start | bytes 393220
  3.5 28.2 %collective-permute-start = (bf16[128,2432]{1,0:T(8,128)(2,1)S(1)}, bf16[128,2432]{1,0:T(8,128)(2,1)S(1)}, u32[]{:S(2)}, u32[]{:S(2)}) collective-permute-start(bf16[128,2432]{1,0:T(8,128)(2,1)S(1)} %normalize.1.refs_4_), channel_id=1, source_target_pairs={{0,64},{32,480},{64,128},{96,32},{128,192},{160,96},{192,256},{224... | collective-permute-start | bytes 1867784 | tf_op jit(solution)/shard_map/ppermute | solution.py:274
  15.0 20.3 %collective-permute-start.2 = (bf16[128,2432]{1,0:T(8,128)(2,1)S(1)}, bf16[128,2432]{1,0:T(8,128)(2,1)}, u32[]{:S(2)}, u32[]{:S(2)}) collective-permute-start(bf16[128,2432]{1,0:T(8,128)(2,1)S(1)} %normalize.1.refs_4_), channel_id=1, source_target_pairs={{0,448},{32,96},{64,0},{96,160},{128,64},{160,224},{192,128},{224,... | collective-permute-start | bytes 1867784 | tf_op jit(solution)/shard_map/ppermute | solution.py:275
  18.4 23.4 %all-to-all-start = ((bf16[32,48,128]{2,1,0:T(8,128)(2,1)}), bf16[32,48,128]{2,1,0:T(8,128)(2,1)S(1)}, u32[]{:S(2)}, u32[]{:S(2)}) async-start(bf16[32,48,128]{2,1,0:T(8,128)(2,1)} %pack_rows.1), calls=%async_computation | async-start | bytes 786432 | tf_op jit(solution)/shard_map/all_to_all | solution.py:279
  28.1 35.8 %collective-permute-start.1 = (bf16[3,2432,128]{2,1,0:T(8,128)(2,1)}, bf16[3,2432,128]{2,1,0:T(8,128)(2,1)}, u32[]{:S(2)}, u32[]{:S(2)}) collective-permute-start(bf16[3,2432,128]{2,1,0:T(8,128)(2,1)} %bitcast.7.own_ref), channel_id=1, source_target_pairs={{0,32},{32,0},{64,96},{96,64},{128,160},{160,128},{192,224},{224,1... | collective-permute-start | bytes 5603336 | tf_op jit(solution)/shard_map/ppermute | solution.py:281
  31.7 32.2 %copy-start.8 = (bf16[128,2432]{1,0:T(8,128)(2,1)}, bf16[128,2432]{1,0:T(8,128)(2,1)S(1)}, u32[]{:S(2)}) copy-start(bf16[128,2432]{1,0:T(8,128)(2,1)S(1)} %collective-permute-done.refs_5_) | copy-start | bytes 1867780
  31.7 27.5 %collective-permute-start.3 = (bf16[128,2432]{1,0:T(8,128)(2,1)S(1)}, bf16[128,2432]{1,0:T(8,128)(2,1)}, u32[]{:S(2)}, u32[]{:S(2)}) collective-permute-start(bf16[128,2432]{1,0:T(8,128)(2,1)S(1)} %collective-permute-done.refs_5_), channel_id=1, source_target_pairs={{0,64},{32,480},{64,128},{96,32},{128,192},{160,96},{192,256},{224... | collective-permute-start | bytes 1867784 | tf_op jit(solution)/shard_map/ppermute | solution.py:282
  35.4 21.9 %collective-permute-start.4 = (bf16[128,2432]{1,0:T(8,128)(2,1)}, bf16[128,2432]{1,0:T(8,128)(2,1)}, u32[]{:S(2)}, u32[]{:S(2)}) collective-permute-start(bf16[128,2432]{1,0:T(8,128)(2,1)} %collective-permute-done.2.refs_6_), channel_id=1, source_target_pairs={{0,448},{32,96},{64,0},{96,160},{128,64},{160,224},{192,128},{224,... | collective-permute-start | bytes 1867784 | tf_op jit(solution)/shard_map/ppermute | solution.py:283
  41.8 15.0 %copy-start.10 = (bf16[32,48,128]{2,1,0:T(8,128)(2,1)}, bf16[32,48,128]{2,1,0:T(8,128)(2,1)S(1)}, u32[]{:S(2)}) copy-start(bf16[32,48,128]{2,1,0:T(8,128)(2,1)S(1)} %all-to-all-done) | copy-start | bytes 1179652
  43.0 13.7 %all-to-all-start.1 = ((f32[32,1,152]{2,1,0:T(1,128)}), f32[32,1,152]{2,1,0:T(1,128)S(1)}, u32[]{:S(2)}, u32[]{:S(2)}) async-start(f32[32,1,152]{2,1,0:T(1,128)} %copy.14), calls=%async_computation.1 | async-start | bytes 65536 | tf_op jit(solution)/shard_map/all_to_all | solution.py:294
  57.3 26.0 %collective-permute-start.7 = (bf16[128,2432]{1,0:T(8,128)(2,1)}, bf16[128,2432]{1,0:T(8,128)(2,1)}, u32[]{:S(2)}, u32[]{:S(2)}) collective-permute-start(bf16[128,2432]{1,0:T(8,128)(2,1)} %collective-permute-done.4.refs_8_), channel_id=1, source_target_pairs={{0,448},{32,96},{64,0},{96,160},{128,64},{160,224},{192,128},{224,... | collective-permute-start | bytes 1867784 | tf_op jit(solution)/shard_map/ppermute | solution.py:295
  59.2 19.1 %collective-permute-start.6 = (bf16[128,2432]{1,0:T(8,128)(2,1)}, bf16[128,2432]{1,0:T(8,128)(2,1)}, u32[]{:S(2)}, u32[]{:S(2)}) collective-permute-start(bf16[128,2432]{1,0:T(8,128)(2,1)} %collective-permute-done.3.refs_7_), channel_id=1, source_target_pairs={{0,64},{32,480},{64,128},{96,32},{128,192},{160,96},{192,256},{224... | collective-permute-start | bytes 1867784 | tf_op jit(solution)/shard_map/ppermute | solution.py:293
  63.9 3.2 %copy-start.9 = (bf16[128,2432]{1,0:T(8,128)(2,1)S(1)}, bf16[128,2432]{1,0:T(8,128)(2,1)}, u32[]{:S(2)}) copy-start(bf16[128,2432]{1,0:T(8,128)(2,1)} %copy-done.8) | copy-start | bytes 1867780
  67.2 5.9 %copy-start.1 = (bf16[2432,768]{1,0:T(8,128)(2,1)}, bf16[2432,768]{1,0:T(8,128)(2,1)S(1)}, u32[]{:S(2)}) copy-start(bf16[2432,768]{1,0:T(8,128)(2,1)S(1)} %get-tuple-element.24.refs_0_) | copy-start | bytes 11206660
  73.1 10.2 %collective-permute-start.5 = (bf16[640,384]{1,0:T(8,128)(2,1)S(1)}, bf16[640,384]{1,0:T(8,128)(2,1)S(1)}, u32[]{:S(2)}, u32[]{:S(2)}) collective-permute-start(bf16[640,384]{1,0:T(8,128)(2,1)S(1)} %get-tuple-element.27), channel_id=1, source_target_pairs={{0,32},{32,0},{64,96},{96,64},{128,160},{160,128},{192,224},{224,1... | collective-permute-start | bytes 1474568 | tf_op jit(solution)/shard_map/ppermute | solution.py:302
  78.4 12.3 %collective-permute-start.9 = (bf16[128,2432]{1,0:T(8,128)(2,1)}, bf16[128,2432]{1,0:T(8,128)(2,1)S(1)}, u32[]{:S(2)}, u32[]{:S(2)}) collective-permute-start(bf16[128,2432]{1,0:T(8,128)(2,1)} %collective-permute-done.6.refs_6_), channel_id=1, source_target_pairs={{0,64},{32,480},{64,128},{96,32},{128,192},{160,96},{192,256},{224... | collective-permute-start | bytes 1867784 | tf_op jit(solution)/shard_map/ppermute | solution.py:303
  83.3 2.1 %copy-start.2 = (bf16[2432,768]{1,0:T(8,128)(2,1)S(1)}, bf16[2432,768]{1,0:T(8,128)(2,1)}, u32[]{:S(2)}) copy-start(bf16[2432,768]{1,0:T(8,128)(2,1)} %copy-done.1) | copy-start | bytes 11206660
  88.3 3.3 %collective-permute-start.8 = (bf16[256,384]{1,0:T(8,128)(2,1)S(1)}, bf16[256,384]{1,0:T(8,128)(2,1)S(1)}, u32[]{:S(2)}, u32[]{:S(2)}) collective-permute-start(bf16[256,384]{1,0:T(8,128)(2,1)S(1)} %get-tuple-element.30), channel_id=1, source_target_pairs={{0,32},{32,0},{64,96},{96,64},{128,160},{160,128},{192,224},{224,1... | collective-permute-start | bytes 589832 | tf_op jit(solution)/shard_map/ppermute | solution.py:307
  92.6 3.9 %collective-permute-start.10 = (bf16[128,384]{1,0:T(8,128)(2,1)S(1)}, bf16[128,384]{1,0:T(8,128)(2,1)S(1)}, u32[]{:S(2)}, u32[]{:S(2)}) collective-permute-start(bf16[128,384]{1,0:T(8,128)(2,1)S(1)} %get-tuple-element.34), channel_id=1, source_target_pairs={{0,32},{32,0},{64,96},{96,64},{128,160},{160,128},{192,224},{224,1... | collective-permute-start | bytes 294920 | tf_op jit(solution)/shard_map/ppermute | solution.py:309
